TPU v7x, 32 devices: a whole 2x2x4 slice. The times are simulated.
32 devices in a mesh: fsdp: 4 (over y, x), ctx: 8 (over z, core).
Axes of the slice: x: 2, y: 2, z: 4, core: 2. Of those that a mesh axis runs over, the one named last changes fastest.
Arguments:
- hidden_in: bfloat16 [4, 2048, 1024], P('fsdp', 'ctx'), may hold values from -6 to 6
- teacher: bfloat16 [4, 2048, 1024], P('fsdp', 'ctx'), may hold values from -8 to 8
- valid: int32 [4, 2048], P('fsdp', 'ctx'), may hold values from 0 to 1, as said below
- positions: int32 [4, 2048], P('fsdp', 'ctx'), may hold values from 0 to 3071, as said below
- norm_attn: bfloat16 [1024], P('fsdp'), may hold values from 0.5 to 1.5
- w_query: bfloat16 [1024, 2048], P('fsdp'), may hold values from -0.1875 to 0.1875
- key_projection: bfloat16 [1024, 1024], P('fsdp'), may hold values from -0.1875 to 0.1875
- value_projection: bfloat16 [1024, 1024], P('fsdp'), may hold values from -0.1875 to 0.1875
- gain_query: bfloat16 [128], P('fsdp'), may hold values from 0.5 to 1.5
- gain_key: bfloat16 [128], P('fsdp'), may hold values from 0.5 to 1.5
- w_out: bfloat16 [2048, 1024], P('fsdp'), may hold values from -3 to 3
- norm_mlp: bfloat16 [1024], P('fsdp'), may hold values from 0.5 to 1.5
- w_gate: bfloat16 [1024, 3072], P('fsdp'), may hold values from -0.1875 to 0.1875
- w_up: bfloat16 [1024, 3072], P('fsdp'), may hold values from -0.1875 to 0.1875
- w_down: bfloat16 [3072, 1024], P('fsdp'), may hold values from -0.109375 to 0.109375
Outputs:
- output: bfloat16 [4, 2048, 1024], P('fsdp', 'ctx')
- loss: float32 [], replicated
- input_grad: float32 [4, 2048, 1024], P('fsdp', 'ctx')
- grad_norm_attn: float32 [1024], P('fsdp')
- grad_w_query: float32 [1024, 2048], P('fsdp')
- grad_w_key: float32 [1024, 1024], P('fsdp')
- grad_w_value: float32 [1024, 1024], P('fsdp')
- grad_gain_query: float32 [128], P('fsdp')
- grad_gain_key: float32 [128], P('fsdp')
- grad_w_out: float32 [2048, 1024], P('fsdp')
- grad_norm_mlp: float32 [1024], P('fsdp')
- grad_w_gate: float32 [1024, 3072], P('fsdp')
- grad_w_up: float32 [1024, 3072], P('fsdp')
- grad_w_down: float32 [3072, 1024], P('fsdp')
Inputs may be any that keep to these rules, and one draw needn't show every extreme that they name: `valid`: 1 marks a token that the loss counts. positions start at 0 in each sequence and rise by 1 or 2 from token to token, by 2 at exactly 1024 of the steps.
All inputs are finite; a program needn't handle non-finite values.
Results may differ from a plain program's by a relative error of at most 0.028.
Values may be sent and summed in bfloat16 or wider, within the bound.
A program may use at most 192 MiB of HBM per device.

v0:
```python
from functools import partial
import math

import jax
import jax.numpy as jnp
from jax import lax
from jax.sharding import PartitionSpec as P

QUERY_HEADS = 16
KEY_VALUE_HEADS = 8
HEAD_SIZE = 128


EPSILON = 1e-06


def root_mean_norm(values, norm_gain):
    return (
        values * lax.rsqrt(jnp.mean(values * values, axis=-1, keepdims=True) + EPSILON) * norm_gain
    )


def rope_tables(position_ids):
    half_width = HEAD_SIZE // 2
    freq_table = jnp.exp(
        jnp.arange(half_width, dtype=jnp.float32) * (-2.0 * math.log(1000000.0) / HEAD_SIZE)
    )
    angle_table = position_ids.astype(jnp.float32)[:, None] * freq_table[None, :]
    cosine_table = jnp.cos(angle_table)
    sine_table = jnp.sin(angle_table)
    return (
        jnp.concatenate([cosine_table, cosine_table], -1),
        jnp.concatenate([-sine_table, sine_table], -1),
    )


def apply_rotary(values, cosine_table, sine_table):
    half_width = HEAD_SIZE // 2
    swapped = jnp.concatenate([values[..., half_width:], values[..., :half_width]], -1)
    return values * cosine_table[:, None, :] + swapped * sine_table[:, None, :]


def shape_heads(cosine_table, sine_table, proj_query, projected_key, gain_q, key_gain):
    token_rows = proj_query.shape[0]
    query_rows = apply_rotary(
        root_mean_norm(proj_query.reshape(token_rows, QUERY_HEADS, HEAD_SIZE), gain_q),
        cosine_table,
        sine_table,
    )
    rows_of_keys = apply_rotary(
        root_mean_norm(projected_key.reshape(token_rows, KEY_VALUE_HEADS, HEAD_SIZE), key_gain),
        cosine_table,
        sine_table,
    )
    return (query_rows, rows_of_keys)


def swiglu(gate_proj, up_proj):
    return gate_proj / (1.0 + jnp.exp(-gate_proj)) * up_proj


def contract_rows(left_arr, right_arr):
    return lax.dot_general(
        left_arr, right_arr, (((0,), (0,)), ((), ())), preferred_element_type=jnp.float32
    )


def against(left_arr, right_arr):
    return lax.dot_general(
        left_arr, right_arr, (((1,), (1,)), ((), ())), preferred_element_type=jnp.float32
    )


def in_blocks(block_step, running, shard_portion):
    total_rows = shard_portion.shape[0]
    block_extent = 512
    block_count = total_rows // block_extent
    blocks = shard_portion.reshape((block_count, block_extent) + shard_portion.shape[1:])
    starts = jnp.arange(block_count, dtype=jnp.int32) * block_extent

    def scan_body(state, scan_item):
        return (block_step(state, scan_item[0], scan_item[1]), None)

    running, unused = lax.scan(scan_body, running, (blocks, starts))
    return running


def score_terms(
    query_rows,
    output_gradients,
    lse_heads,
    delta_heads,
    rows_of_keys,
    rows_of_values,
    query_index,
    key_index,
    score_scale,
):
    score_matrix = (
        jnp.einsum("alci,wli->lcaw", query_rows, rows_of_keys, preferred_element_type=jnp.float32)
        * score_scale
    )
    allowed = key_index[None, :] <= query_index[:, None]
    attention_probabilities = jnp.where(allowed, jnp.exp(score_matrix - lse_heads[..., None]), 0.0)
    grad_probs = jnp.einsum(
        "alci,wli->lcaw", output_gradients, rows_of_values, preferred_element_type=jnp.float32
    )
    score_gradient = (
        score_scale * attention_probabilities * (grad_probs - delta_heads[..., None])
    ).astype(jnp.bfloat16)
    return (attention_probabilities, score_gradient)


def per_device(
    hidden_in,
    teacher,
    valid,
    positions,
    norm_attn,
    w_query,
    key_projection,
    value_projection,
    gain_query,
    gain_key,
    w_out,
    norm_mlp,
    w_gate,
    w_up,
    w_down,
):
    gathered = (
        lax.all_gather(norm_attn, "fsdp", axis=0, tiled=True),
        lax.all_gather(w_query, "fsdp", axis=0, tiled=True),
        lax.all_gather(key_projection, "fsdp", axis=0, tiled=True),
        lax.all_gather(value_projection, "fsdp", axis=0, tiled=True),
        lax.all_gather(gain_query, "fsdp", axis=0, tiled=True),
        lax.all_gather(gain_key, "fsdp", axis=0, tiled=True),
        lax.all_gather(w_out, "fsdp", axis=0, tiled=True),
        lax.all_gather(norm_mlp, "fsdp", axis=0, tiled=True),
        lax.all_gather(w_gate, "fsdp", axis=0, tiled=True),
        lax.all_gather(w_up, "fsdp", axis=0, tiled=True),
        lax.all_gather(w_down, "fsdp", axis=0, tiled=True),
    )
    (
        full_norm_attn,
        full_query,
        full_key,
        full_value,
        full_gain_q,
        full_gain_k,
        full_out,
        full_norm_mlp,
        full_gate,
        full_up,
        full_down,
    ) = gathered
    grouped_heads = QUERY_HEADS // KEY_VALUE_HEADS
    score_scale = 1.0 / math.sqrt(HEAD_SIZE)
    residual = hidden_in[0].astype(jnp.float32)
    token_rows = residual.shape[0]
    query_index = lax.axis_index("ctx") * token_rows + jnp.arange(token_rows, dtype=jnp.int32)
    normed_one, norm_one_back = jax.vjp(
        root_mean_norm, residual, full_norm_attn.astype(jnp.float32)
    )
    hidden_one = normed_one.astype(jnp.bfloat16)
    proj_query = jnp.dot(hidden_one, full_query, preferred_element_type=jnp.float32)
    projected_key = jnp.dot(hidden_one, full_key, preferred_element_type=jnp.float32)
    projected_value = jnp.dot(hidden_one, full_value, preferred_element_type=jnp.float32)
    cosine_table, sine_table = rope_tables(positions[0])
    (query_per_head, heads_key), heads_back = jax.vjp(
        partial(shape_heads, cosine_table, sine_table),
        proj_query,
        projected_key,
        full_gain_q.astype(jnp.float32),
        full_gain_k.astype(jnp.float32),
    )
    query_reduced = query_per_head.astype(jnp.bfloat16).reshape(
        token_rows, KEY_VALUE_HEADS, grouped_heads, HEAD_SIZE
    )
    key_reduced = heads_key.astype(jnp.bfloat16)
    value_reduced = projected_value.astype(jnp.bfloat16).reshape(
        token_rows, KEY_VALUE_HEADS, HEAD_SIZE
    )
    key_value = jnp.stack(
        [
            key_reduced.reshape(token_rows, KEY_VALUE_HEADS * HEAD_SIZE),
            value_reduced.reshape(token_rows, KEY_VALUE_HEADS * HEAD_SIZE),
        ],
        axis=1,
    )

    def forward_block(running, shard_portion, first_row):
        run_max, run_total, run_acc = running
        rows_per_block = shard_portion.shape[0]
        rows_of_keys = shard_portion[:, 0].reshape(rows_per_block, KEY_VALUE_HEADS, HEAD_SIZE)
        rows_of_values = shard_portion[:, 1].reshape(rows_per_block, KEY_VALUE_HEADS, HEAD_SIZE)
        key_index = first_row + jnp.arange(rows_per_block, dtype=jnp.int32)
        allowed = key_index[None, :] <= query_index[:, None]
        score_matrix = (
            jnp.einsum(
                "alci,wli->lcaw", query_reduced, rows_of_keys, preferred_element_type=jnp.float32
            )
            * score_scale
        )
        score_matrix = jnp.where(allowed, score_matrix, -1e30)
        new_max = jnp.maximum(run_max, jnp.max(score_matrix, axis=-1))
        weights_part = jnp.where(allowed, jnp.exp(score_matrix - new_max[..., None]), 0.0)
        factor = jnp.exp(run_max - new_max)
        run_total = run_total * factor + jnp.sum(weights_part, axis=-1)
        run_acc = run_acc * factor[..., None] + jnp.einsum(
            "exfw,weq->exfq",
            weights_part.astype(jnp.bfloat16),
            rows_of_values,
            preferred_element_type=jnp.float32,
        )
        return (new_max, run_total, run_acc)

    start_state = (
        jnp.full((KEY_VALUE_HEADS, grouped_heads, token_rows), -1e30, jnp.float32),
        jnp.zeros((KEY_VALUE_HEADS, grouped_heads, token_rows), jnp.float32),
        jnp.zeros((KEY_VALUE_HEADS, grouped_heads, token_rows, HEAD_SIZE), jnp.float32),
    )
    run_max, run_total, run_acc = in_blocks(
        forward_block, start_state, lax.all_gather(key_value, "ctx", axis=0, tiled=True)
    )
    log_total = run_max + jnp.log(run_total)
    attn_rows = jnp.transpose(run_acc / run_total[..., None], (2, 0, 1, 3))
    attn_low = attn_rows.reshape(token_rows, QUERY_HEADS * HEAD_SIZE).astype(jnp.bfloat16)
    mid_resid = residual + jnp.dot(attn_low, full_out, preferred_element_type=jnp.float32)
    normed_two, norm_two_back = jax.vjp(
        root_mean_norm, mid_resid, full_norm_mlp.astype(jnp.float32)
    )
    hidden_two = normed_two.astype(jnp.bfloat16)
    gate_proj = jnp.dot(hidden_two, full_gate, preferred_element_type=jnp.float32)
    up_proj = jnp.dot(hidden_two, full_up, preferred_element_type=jnp.float32)
    gated, gated_back = jax.vjp(swiglu, gate_proj, up_proj)
    gated_low = gated.astype(jnp.bfloat16)
    final_rows = mid_resid + jnp.dot(gated_low, full_down, preferred_element_type=jnp.float32)
    target = teacher[0].astype(jnp.float32)
    weight_rows = valid[0].astype(jnp.float32)
    mismatch = final_rows - target
    sq_local = jnp.sum(weight_rows[:, None] * mismatch * mismatch)
    count_local = jnp.sum(weight_rows)
    sq_total, count_total = lax.psum((sq_local, count_local), ("fsdp", "ctx"))
    loss_value = sq_total / count_total
    loss_scale = token_rows * lax.axis_size("ctx") * lax.axis_size("fsdp") / 4.0
    grad_final = 2.0 * loss_scale / count_total * weight_rows[:, None] * mismatch
    grad_down_in = grad_final.astype(jnp.bfloat16)
    grad_w_down = contract_rows(gated_low, grad_down_in)
    grad_gated = against(grad_down_in, full_down)
    grad_gate_proj, grad_up_proj = gated_back(grad_gated)
    gate_low = grad_gate_proj.astype(jnp.bfloat16)
    up_low = grad_up_proj.astype(jnp.bfloat16)
    grad_w_gate = contract_rows(hidden_two, gate_low)
    grad_w_up = contract_rows(hidden_two, up_low)
    grad_hidden_two = against(gate_low, full_gate) + against(up_low, full_up)
    grad_mid_norm, grad_norm_mlp = norm_two_back(grad_hidden_two)
    grad_mid = grad_final + grad_mid_norm
    grad_branch = grad_mid.astype(jnp.bfloat16)
    grad_w_out = contract_rows(attn_low, grad_branch)
    attention_gradient = against(grad_branch, full_out).astype(jnp.bfloat16)
    attention_head_gradient = attention_gradient.reshape(
        token_rows, KEY_VALUE_HEADS, grouped_heads, HEAD_SIZE
    )
    row_delta = jnp.sum(attention_head_gradient.astype(jnp.float32) * attn_rows, axis=-1)
    delta_heads = jnp.transpose(row_delta, (1, 2, 0))
    row_stats = jnp.stack(
        [
            jnp.transpose(log_total, (2, 0, 1)).reshape(token_rows, QUERY_HEADS),
            row_delta.reshape(token_rows, QUERY_HEADS),
        ],
        axis=1,
    )

    def block_of_queries(grad_query, shard_portion, first_row):
        rows_per_block = shard_portion.shape[0]
        rows_of_keys = shard_portion[:, 0].reshape(rows_per_block, KEY_VALUE_HEADS, HEAD_SIZE)
        rows_of_values = shard_portion[:, 1].reshape(rows_per_block, KEY_VALUE_HEADS, HEAD_SIZE)
        key_index = first_row + jnp.arange(rows_per_block, dtype=jnp.int32)
        attention_probabilities, score_gradient = score_terms(
            query_reduced,
            attention_head_gradient,
            log_total,
            delta_heads,
            rows_of_keys,
            rows_of_values,
            query_index,
            key_index,
            score_scale,
        )
        return grad_query + jnp.einsum(
            "jyux,xji->ujyi", score_gradient, rows_of_keys, preferred_element_type=jnp.float32
        )

    grad_query = in_blocks(
        block_of_queries,
        jnp.zeros((token_rows, KEY_VALUE_HEADS, grouped_heads, HEAD_SIZE), jnp.float32),
        lax.all_gather(key_value, "ctx", axis=0, tiled=True),
    )
    all_stats = lax.all_gather(row_stats.astype(jnp.bfloat16), "ctx", axis=0, tiled=True).astype(
        row_stats.dtype
    )
    query_pair = jnp.stack(
        [query_reduced.reshape(token_rows, QUERY_HEADS * HEAD_SIZE), attention_gradient], axis=1
    )

    def key_block(running, shard_portion, first_row):
        grad_key, value_gradient = running
        rows_per_block = shard_portion.shape[0]
        query_rows = shard_portion[:, 0].reshape(
            rows_per_block, KEY_VALUE_HEADS, grouped_heads, HEAD_SIZE
        )
        output_gradients = shard_portion[:, 1].reshape(
            rows_per_block, KEY_VALUE_HEADS, grouped_heads, HEAD_SIZE
        )
        partial_statistics = lax.dynamic_slice_in_dim(all_stats, first_row, rows_per_block, 0)
        partial_logsumexp = jnp.transpose(
            partial_statistics[:, 0].reshape(rows_per_block, KEY_VALUE_HEADS, grouped_heads),
            (1, 2, 0),
        )
        partial_delta = jnp.transpose(
            partial_statistics[:, 1].reshape(rows_per_block, KEY_VALUE_HEADS, grouped_heads),
            (1, 2, 0),
        )
        part_index = first_row + jnp.arange(rows_per_block, dtype=jnp.int32)
        attention_probabilities, score_gradient = score_terms(
            query_rows,
            output_gradients,
            partial_logsumexp,
            partial_delta,
            key_reduced,
            value_reduced,
            part_index,
            query_index,
            score_scale,
        )
        grad_key = grad_key + jnp.einsum(
            "wzlj,lwzy->jwy", score_gradient, query_rows, preferred_element_type=jnp.float32
        )
        value_gradient = value_gradient + jnp.einsum(
            "wzlj,lwzy->jwy",
            attention_probabilities.astype(jnp.bfloat16),
            output_gradients,
            preferred_element_type=jnp.float32,
        )
        return (grad_key, value_gradient)

    key_state = (
        jnp.zeros((token_rows, KEY_VALUE_HEADS, HEAD_SIZE), jnp.float32),
        jnp.zeros((token_rows, KEY_VALUE_HEADS, HEAD_SIZE), jnp.float32),
    )
    grad_key, value_gradient = in_blocks(
        key_block, key_state, lax.all_gather(query_pair, "ctx", axis=0, tiled=True)
    )
    grad_proj_q, grad_proj_k, grad_gain_q, grad_gain_k = heads_back(
        (grad_query.reshape(token_rows, QUERY_HEADS, HEAD_SIZE), grad_key)
    )
    query_grad_low = grad_proj_q.astype(jnp.bfloat16)
    key_grad_low = grad_proj_k.astype(jnp.bfloat16)
    value_gradient_reduced = value_gradient.reshape(token_rows, KEY_VALUE_HEADS * HEAD_SIZE).astype(
        jnp.bfloat16
    )
    grad_w_query = contract_rows(hidden_one, query_grad_low)
    grad_w_key = contract_rows(hidden_one, key_grad_low)
    grad_w_value = contract_rows(hidden_one, value_gradient_reduced)
    grad_hidden_one = (
        against(query_grad_low, full_query)
        + against(key_grad_low, full_key)
        + against(value_gradient_reduced, full_value)
    )
    grad_resid_norm, grad_norm_attn = norm_one_back(grad_hidden_one)
    grad_input = grad_mid + grad_resid_norm
    grads = (
        grad_norm_attn,
        grad_w_query,
        grad_w_key,
        grad_w_value,
        grad_gain_q,
        grad_gain_k,
        grad_w_out,
        grad_norm_mlp,
        grad_w_gate,
        grad_w_up,
        grad_w_down,
    )
    shares = (
        lax.psum_scatter(grads[0], ("fsdp", "ctx"), scatter_dimension=0, tiled=True),
        lax.psum_scatter(grads[1], ("fsdp", "ctx"), scatter_dimension=0, tiled=True),
        lax.psum_scatter(grads[2], ("fsdp", "ctx"), scatter_dimension=0, tiled=True),
        lax.psum_scatter(grads[3], ("fsdp", "ctx"), scatter_dimension=0, tiled=True),
        lax.psum_scatter(grads[4], ("fsdp", "ctx"), scatter_dimension=0, tiled=True),
        lax.psum_scatter(grads[5], ("fsdp", "ctx"), scatter_dimension=0, tiled=True),
        lax.psum_scatter(grads[6], ("fsdp", "ctx"), scatter_dimension=0, tiled=True),
        lax.psum_scatter(grads[7], ("fsdp", "ctx"), scatter_dimension=0, tiled=True),
        lax.psum_scatter(grads[8], ("fsdp", "ctx"), scatter_dimension=0, tiled=True),
        lax.psum_scatter(grads[9], ("fsdp", "ctx"), scatter_dimension=0, tiled=True),
        lax.psum_scatter(grads[10], ("fsdp", "ctx"), scatter_dimension=0, tiled=True),
    )
    shares = (
        lax.all_gather(shares[0].astype(jnp.bfloat16), "ctx", axis=0, tiled=True).astype(
            jnp.float32
        ),
        lax.all_gather(shares[1].astype(jnp.bfloat16), "ctx", axis=0, tiled=True).astype(
            jnp.float32
        ),
        lax.all_gather(shares[2].astype(jnp.bfloat16), "ctx", axis=0, tiled=True).astype(
            jnp.float32
        ),
        lax.all_gather(shares[3].astype(jnp.bfloat16), "ctx", axis=0, tiled=True).astype(
            jnp.float32
        ),
        lax.all_gather(shares[4].astype(jnp.bfloat16), "ctx", axis=0, tiled=True).astype(
            jnp.float32
        ),
        lax.all_gather(shares[5].astype(jnp.bfloat16), "ctx", axis=0, tiled=True).astype(
            jnp.float32
        ),
        lax.all_gather(shares[6].astype(jnp.bfloat16), "ctx", axis=0, tiled=True).astype(
            jnp.float32
        ),
        lax.all_gather(shares[7].astype(jnp.bfloat16), "ctx", axis=0, tiled=True).astype(
            jnp.float32
        ),
        lax.all_gather(shares[8].astype(jnp.bfloat16), "ctx", axis=0, tiled=True).astype(
            jnp.float32
        ),
        lax.all_gather(shares[9].astype(jnp.bfloat16), "ctx", axis=0, tiled=True).astype(
            jnp.float32
        ),
        lax.all_gather(shares[10].astype(jnp.bfloat16), "ctx", axis=0, tiled=True).astype(
            jnp.float32
        ),
    )
    return (
        final_rows.astype(jnp.bfloat16)[None],
        loss_value,
        grad_input[None],
        shares[0],
        shares[1],
        shares[2],
        shares[3],
        shares[4],
        shares[5],
        shares[6],
        shares[7],
        shares[8],
        shares[9],
        shares[10],
    )


def solution(mesh):
    return jax.shard_map(
        per_device,
        mesh=mesh,
        in_specs=(
            P("fsdp", "ctx", None),
            P("fsdp", "ctx", None),
            P("fsdp", "ctx"),
            P("fsdp", "ctx"),
            P("fsdp"),
            P("fsdp", None),
            P("fsdp", None),
            P("fsdp", None),
            P("fsdp"),
            P("fsdp"),
            P("fsdp", None),
            P("fsdp"),
            P("fsdp", None),
            P("fsdp", None),
            P("fsdp", None),
        ),
        out_specs=(
            P("fsdp", "ctx", None),
            P(),
            P("fsdp", "ctx", None),
            P("fsdp"),
            P("fsdp", None),
            P("fsdp", None),
            P("fsdp", None),
            P("fsdp"),
            P("fsdp"),
            P("fsdp", None),
            P("fsdp"),
            P("fsdp", None),
            P("fsdp", None),
            P("fsdp", None),
        ),
        check_vma=False,
    )
```

profile of v0, /device:TPU:0, one launch (start us, length us, event | category | flops | bytes accessed | tf_op | source)
XLA Modules:
  0.0 2012.5 jit_solution(12352168647764285354)
XLA Ops:
  10.1 9.5 all-gather
  23.3 8.9 all-reduce.16
  33.5 14.5 all-gather.17.cloned.1.call-done
  55.6 29.6 %all-gather.19.cloned.1.call-done = bf16[1024,1024]{1,0:T(8,128)(2,1)} async-done(((bf16[256,1024]{1,0:T(8,128)(2,1)}), bf16[1024,1024]{1,0:T(8,128)(2,1)}) %all-gather.19.cloned.1.call-update) | async-done | bytes 2097168 | tf_op jit(solution)/shard_map/all_gather | solution.py:135
  92.1 8.0 all-gather.1
  100.1 40.1 %psum.15 = f32[]{:T(128)} all-reduce(f32[]{:T(128)} %convert_reduce_fusion), channel_id=1, replica_groups=mesh['fsdp'=4,'ctx'=8] {'fsdp','ctx'}, use_global_device_ids=true, to_apply=%region_11.12 | all-reduce | flops 1 | bytes 8 | tf_op jit(solution)/shard_map/psum | solution.py:244
  141.0 6.4 copy.117
  153.7 71.3 %all-gather.21.cloned.1.call-done = bf16[2048,2,1024]{2,0,1:T(8,128)(2,1)} async-done(((bf16[256,2,1024]{2,0,1:T(8,128)(2,1)}), bf16[2048,2,1024]{2,0,1:T(8,128)(2,1)}) %all-gather.21.cloned.1.call-update) | async-done | bytes 8388624 | tf_op jit(solution)/shard_map/all_gather | solution.py:224
  225.1 11.7 copy.118
  236.8 77.4 %while.39 = (s32[]{:T(128)}, f32[8,2,256]{2,1,0:T(2,128)S(1)}, f32[8,2,256]{2,1,0:T(2,128)S(1)}, f32[8,2,256,128]{3,2,1,0:T(8,128)}, s32[4]{0:T(128)S(1)}, /*ind...) while((s32[]{:T(128)}, f32[8,2,256]{2,1,0:T(2,128)S(1)}, ...), condition=%wide.region_6.7_spmd.clone, body=%wide.region_3.6_spmd.clone.sunk | while | flops 1102729984 | bytes 75241640 | solution.py:84
  240.1 4.9 fusion.219
  258.2 4.9 fusion.219
  269.0 5.3 fusion.223
  277.6 4.9 fusion.219
  289.3 5.6 fusion.223
  298.2 4.9 fusion.219
  308.9 5.3 fusion.223
  324.7 25.2 %all-gather.27.cloned.1.call-done = bf16[1024,3072]{1,0:T(8,128)(2,1)} async-done(((bf16[256,3072]{1,0:T(8,128)(2,1)}), bf16[1024,3072]{1,0:T(8,128)(2,1)}) %all-gather.27.cloned.1.call-update) | async-done | bytes 6291472 | tf_op jit(solution)/shard_map/all_gather | solution.py:140
  350.0 6.2 fusion.131
  356.2 65.8 %all-gather.29.cloned.1.call-done = bf16[1024,3072]{1,0:T(8,128)(2,1)} async-done(((bf16[256,3072]{1,0:T(8,128)(2,1)}), bf16[1024,3072]{1,0:T(8,128)(2,1)}) %all-gather.29.cloned.1.call-update) | async-done | bytes 6291472 | tf_op jit(solution)/shard_map/all_gather | solution.py:141
  422.0 8.0 multiply_convert_fusion.1
  430.0 64.1 %all-gather.31.cloned.1.call-done = bf16[3072,1024]{1,0:T(8,128)(2,1)} async-done(((bf16[768,1024]{1,0:T(8,128)(2,1)}), bf16[3072,1024]{1,0:T(8,128)(2,1)}) %all-gather.31.cloned.1.call-update) | async-done | bytes 6291472 | tf_op jit(solution)/shard_map/all_gather | solution.py:142
  494.0 5.2 multiply_convert_fusion.3
  499.3 9.8 multiply_convert_fusion
  530.3 68.0 %while.40 = (s32[]{:T(128)}, f32[256,8,2,128]{0,3,2,1:T(8,128)}, bf16[4,512,2,1024]{1,3,2,0:T(8,128)(2,1)}, s32[4]{0:T(128)S(1)}, bf16[256,8,2,128]{3,0,2,1:T(8,...) while((s32[]{:T(128)}, f32[256,8,2,128]{0,3,2,1:T(8,128)}, ...), condition=%wide.region_15.16_spmd.clone, body=%wide.region_14.15_spmd.clone.sunk | while | flops 1626473216 | bytes 34904212 | solution.py:84
  538.4 8.6 bitcast_add_fusion.2
  554.9 9.2 bitcast_add_fusion.2
  572.0 9.2 bitcast_add_fusion.2
  589.1 9.2 bitcast_add_fusion.2
  605.4 4.8 fusion.101
  617.9 6.4 fusion.134
  625.7 6.4 fusion.135
  633.7 6.4 fusion.136
  643.6 119.2 %reduce-scatter.8.cloned.1.call-done = f32[32,2048]{1,0:T(8,128)} async-done(((f32[1024,2048]{1,0:T(8,128)}), f32[32,2048]{1,0:T(8,128)}) %reduce-scatter.8.cloned.1.call-update) | async-done | bytes 262160 | tf_op jit(solution)/shard_map/reduce_scatter | solution.py:388
  764.4 150.5 %reduce-scatter.14.cloned.1.call-done = f32[64,1024]{1,0:T(8,128)} async-done(((f32[2048,1024]{1,0:T(8,128)}), f32[64,1024]{1,0:T(8,128)}) %reduce-scatter.14.cloned.1.call-update) | async-done | bytes 262160 | tf_op jit(solution)/shard_map/reduce_scatter | solution.py:393
  916.6 157.6 %reduce-scatter.16.cloned.1.call-done = f32[32,3072]{1,0:T(8,128)} async-done(((f32[1024,3072]{1,0:T(8,128)}), f32[32,3072]{1,0:T(8,128)}) %reduce-scatter.16.cloned.1.call-update) | async-done | bytes 393232 | tf_op jit(solution)/shard_map/reduce_scatter | solution.py:395
  1075.9 159.6 %reduce-scatter.18.cloned.1.call-done = f32[32,3072]{1,0:T(8,128)} async-done(((f32[1024,3072]{1,0:T(8,128)}), f32[32,3072]{1,0:T(8,128)}) %reduce-scatter.18.cloned.1.call-update) | async-done | bytes 393232 | tf_op jit(solution)/shard_map/reduce_scatter | solution.py:396
  1238.6 14.0 all_gather.89
  1252.6 143.5 %reduce-scatter.20.cloned.1.call-done = f32[96,1024]{1,0:T(8,128)} async-done(((f32[3072,1024]{1,0:T(8,128)}), f32[96,1024]{1,0:T(8,128)}) %reduce-scatter.20.cloned.1.call-update) | async-done | bytes 393232 | tf_op jit(solution)/shard_map/reduce_scatter | solution.py:397
  1397.8 150.6 %all-gather.33.cloned.1.call-done = bf16[2048,2,2048]{2,0,1:T(8,128)(2,1)} async-done(((bf16[256,2,2048]{2,0,1:T(8,128)(2,1)}), bf16[2048,2,2048]{2,0,1:T(8,128)(2,1)}) %all-gather.33.cloned.1.call-update) | async-done | bytes 16777232 | tf_op jit(solution)/shard_map/all_gather | solution.py:353
  1548.4 148.9 %while.41 = (s32[]{:T(128)}, f32[256,8,128]{0,2,1:T(8,128)}, f32[256,8,128]{0,2,1:T(8,128)}, bf16[4,512,2,2048]{3,1,0,2:T(8,128)(2,1)}, s32[4]{0:T(128)S(1)}, /*...) while((s32[]{:T(128)}, f32[256,8,128]{0,2,1:T(8,128)}, ...), condition=%wide.region_18.19_spmd.clone, body=%wide.region_17.18_spmd.clone.sunk | while | flops 2171732736 | bytes 64723160 | solution.py:84
  1548.4 4.8 constant_dynamic-slice_fusion.5
  1553.2 6.2 copy.162
  1563.3 4.6 fusion.241
  1571.6 7.5 fusion.242
  1579.0 6.2 fusion.243
  1585.3 4.8 constant_dynamic-slice_fusion.5
  1590.1 6.2 copy.162
  1608.4 7.6 fusion.242
  1616.1 6.5 fusion.243
  1622.6 4.8 constant_dynamic-slice_fusion.5
  1627.4 6.3 copy.162
  1645.8 7.6 fusion.242
  1653.4 6.7 fusion.243
  1660.1 4.8 constant_dynamic-slice_fusion.5
  1664.9 6.2 copy.162
  1683.3 7.6 fusion.242
  1690.9 6.5 fusion.243
  1733.6 39.0 %all-reduce.14 = (f32[]{:T(128)}, bf16[1024]{0:T(1024)(128)(2,1)S(1)}, bf16[128]{0:T(256)(128)(2,1)S(1)}, bf16[128]{0:T(256)(128)(2,1)S(1)}, bf16[1024]{0:T(1024)(128)(2,1)S(1)}) all-reduce(f32[]{:T(128)} %get-tuple-element.479, f32[1024]{0:T(1024)S(1)} %get-tuple-element.391, ...), channel_id=1, replica_groups=mesh['fsdp'=4,'ctx'=8] {'fsdp','ctx'}, use_global_device_ids=true, to_apply=%region_9.10 | all-reduce | flops 2305 | bytes 13832 | tf_op jit(solution)/shard_map/psum | solution.py:244
  1775.0 15.6 all-reduce.15
  1794.1 51.0 %reduce-scatter.10.cloned.1.call-done = f32[32,1024]{1,0:T(8,128)} async-done(((f32[1024,1024]{1,0:T(8,128)}), f32[32,1024]{1,0:T(8,128)}) %reduce-scatter.10.cloned.1.call-update) | async-done | bytes 131088 | tf_op jit(solution)/shard_map/reduce_scatter | solution.py:389
  1846.0 15.3 all_gather.92
  1862.4 124.6 %reduce-scatter.12.cloned.1.call-done = f32[32,1024]{1,0:T(8,128)} async-done(((f32[1024,1024]{1,0:T(8,128)}), f32[32,1024]{1,0:T(8,128)}) %reduce-scatter.12.cloned.1.call-update) | async-done | bytes 131088 | tf_op jit(solution)/shard_map/reduce_scatter | solution.py:390
  1987.9 15.0 all_gather.93
  (440 shorter events, 241.8 us)
Async XLA Ops:
  7.2 26.1 %copy-start.3 = (bf16[1,256,1024]{2,1,0:T(8,128)(2,1)S(1)}, bf16[1,256,1024]{2,1,0:T(8,128)(2,1)}, u32[]{:S(2)}) copy-start(bf16[1,256,1024]{2,1,0:T(8,128)(2,1)} %param.21) | copy-start | bytes 1572868
  7.2 40.8 %all-gather.17.cloned.1.call-start = ((), (), s32[]{:S(2)}) async-start(), calls=%async_computation.7 | async-start | bytes 2621440 | tf_op jit(solution)/shard_map/all_gather | solution.py:134
  7.9 77.2 %all-gather.19.cloned.1.call-start = ((), (), s32[]{:S(2)}) async-start(), calls=%async_computation.8 | async-start | bytes 2621440 | tf_op jit(solution)/shard_map/all_gather | solution.py:135
  8.7 132.3 %all-gather.23.cloned.1.call-start = ((), (), s32[]{:S(2)}) async-start(), calls=%async_computation.10 | async-start | bytes 5242880 | tf_op jit(solution)/shard_map/all_gather | solution.py:133
  9.4 215.7 %all-gather.21.cloned.1.call-start = ((), (), s32[]{:S(2)}) async-start(), calls=%async_computation.9 | async-start | bytes 9437184 | tf_op jit(solution)/shard_map/all_gather | solution.py:224
  19.6 127.8 %copy-start.51 = (f32[4,1,256]{2,1,0:T(1,128)}, f32[4,1,256]{2,1,0:T(1,128)S(1)}, u32[]{:S(2)}) copy-start(f32[4,1,256]{2,1,0:T(1,128)S(1)} %convert_element_type.272) | copy-start | bytes 12292
  32.2 22.5 %copy-start.65 = (f32[128]{0:T(128)}, f32[128]{0:T(128)S(1)}, u32[]{:S(2)}) copy-start(f32[128]{0:T(128)S(1)} %convert_element_type.217) | copy-start | bytes 1540
  33.3 118.5 %copy-start.30 = (f32[256,128]{0,1:T(8,128)}, f32[256,128]{0,1:T(8,128)S(1)}, u32[]{:S(2)}) copy-start(f32[256,128]{0,1:T(8,128)S(1)} %get-tuple-element.500) | copy-start | bytes 393220
  33.3 118.5 %copy-start.33 = (f32[256,128]{0,1:T(8,128)}, f32[256,128]{0,1:T(8,128)S(1)}, u32[]{:S(2)}) copy-start(f32[256,128]{0,1:T(8,128)S(1)} %get-tuple-element.501) | copy-start | bytes 393220
  33.5 20.9 %copy-start.63 = (f32[256]{0:T(256)}, f32[256]{0:T(256)S(1)}, u32[]{:S(2)}) copy-start(f32[256]{0:T(256)S(1)} %fusion.85) | copy-start | bytes 3076
  33.5 113.9 %copy-start.58 = (f32[256]{0:T(256)}, f32[256]{0:T(256)S(1)}, u32[]{:S(2)}) copy-start(f32[256]{0:T(256)S(1)} %fusion.115) | copy-start | bytes 3076
  55.3 33.3 %copy-start.20 = (bf16[256,8,128]{0,2,1:T(8,128)(2,1)}, bf16[256,8,128]{0,2,1:T(8,128)(2,1)S(1)}, u32[]{:S(2)}) copy-start(bf16[256,8,128]{0,2,1:T(8,128)(2,1)S(1)} %fusion.95) | copy-start | bytes 1572868
  87.5 3.1 copy-start.37
  88.7 2.8 copy-start.71
  88.7 3.4 copy-start.73
  88.7 230.9 %all-gather.25.cloned.1.call-start = ((), (), s32[]{:S(2)}) async-start(), calls=%async_computation.11 | async-start | bytes 5242880 | tf_op jit(solution)/shard_map/all_gather | solution.py:138
  89.3 260.7 %all-gather.27.cloned.1.call-start = ((), (), s32[]{:S(2)}) async-start(), calls=%async_computation.12 | async-start | bytes 7864320 | tf_op jit(solution)/shard_map/all_gather | solution.py:140
  89.9 332.1 %all-gather.29.cloned.1.call-start = ((), (), s32[]{:S(2)}) async-start(), calls=%async_computation.13 | async-start | bytes 7864320 | tf_op jit(solution)/shard_map/all_gather | solution.py:141
  90.6 403.4 %all-gather.31.cloned.1.call-start = ((), (), s32[]{:S(2)}) async-start(), calls=%async_computation.14 | async-start | bytes 7864320 | tf_op jit(solution)/shard_map/all_gather | solution.py:142
  91.4 671.3 %reduce-scatter.8.cloned.1.call-start = ((), (), s32[]{:S(2)}) async-start(), calls=%async_computation.16 | async-start | bytes 8650752 | tf_op jit(solution)/shard_map/reduce_scatter | solution.py:388
  92.1 59.7 %copy-start.67 = (f32[128]{0:T(128)}, f32[128]{0:T(128)S(1)}, u32[]{:S(2)}) copy-start(f32[128]{0:T(128)S(1)} %convert_element_type.223) | copy-start | bytes 1540
  153.1 83.8 %copy-start.9 = (bf16[256,16,128]{0,2,1:T(8,128)(2,1)}, bf16[256,16,128]{0,2,1:T(8,128)(2,1)S(1)}, u32[]{:S(2)}) copy-start(bf16[256,16,128]{0,2,1:T(8,128)(2,1)S(1)} %fusion.72) | copy-start | bytes 3145732
  245.0 5.8 copy-start
  263.1 5.8 copy-start
  282.5 6.9 copy-start
  303.1 5.8 copy-start
  319.6 4.0 copy-start.16
  324.7 97.3 %copy-start.18 = (bf16[256,1024]{1,0:T(8,128)(2,1)}, bf16[256,1024]{1,0:T(8,128)(2,1)S(1)}, u32[]{:S(2)}) copy-start(bf16[256,1024]{1,0:T(8,128)(2,1)S(1)} %multiply_convert_fusion.2) | copy-start | bytes 1572868
  356.2 137.8 %copy-start.29 = (f32[256,1024]{1,0:T(8,128)S(1)}, f32[256,1024]{1,0:T(8,128)}, u32[]{:S(2)}) copy-start(f32[256,1024]{1,0:T(8,128)} %copy-done.28) | copy-start | bytes 3145732
  356.2 137.8 %copy-start.48 = (bf16[1,256,1024]{2,1,0:T(8,128)(2,1)S(1)}, bf16[1,256,1024]{2,1,0:T(8,128)(2,1)}, u32[]{:S(2)}) copy-start(bf16[1,256,1024]{2,1,0:T(8,128)(2,1)} %param.22) | copy-start | bytes 1572868
  494.0 5.3 copy-start.75
  494.0 15.1 slice-start
  494.0 17.0 slice-start.2
  499.3 9.8 copy-start.46
  499.3 9.9 slice-start.1
  499.3 11.7 slice-start.3
  513.8 3.0 copy-start.72
  519.1 8.9 copy-start.6
  530.3 68.0 %copy-start.34 = (f32[256,128]{0,1:T(8,128)S(1)}, f32[256,128]{0,1:T(8,128)}, u32[]{:S(2)}) copy-start(f32[256,128]{0,1:T(8,128)} %copy-done.33) | copy-start | bytes 393220
  598.3 2.0 copy-start.31
  598.3 2.0 copy-start.50
  600.1 2.2 copy-start.14
  600.1 2.2 copy-start.68
  610.3 304.6 %reduce-scatter.14.cloned.1.call-start = ((), (), s32[]{:S(2)}) async-start(), calls=%async_computation.20 | async-start | bytes 8650752 | tf_op jit(solution)/shard_map/reduce_scatter | solution.py:393
  616.4 457.8 %reduce-scatter.16.cloned.1.call-start = ((), (), s32[]{:S(2)}) async-start(), calls=%async_computation.22 | async-start | bytes 12976128 | tf_op jit(solution)/shard_map/reduce_scatter | solution.py:395
  624.3 611.2 %reduce-scatter.18.cloned.1.call-start = ((), (), s32[]{:S(2)}) async-start(), calls=%async_computation.24 | async-start | bytes 12976128 | tf_op jit(solution)/shard_map/reduce_scatter | solution.py:396
  632.2 763.9 %reduce-scatter.20.cloned.1.call-start = ((), (), s32[]{:S(2)}) async-start(), calls=%async_computation.26 | async-start | bytes 12976128 | tf_op jit(solution)/shard_map/reduce_scatter | solution.py:397
  640.1 908.3 %all-gather.33.cloned.1.call-start = ((), (), s32[]{:S(2)}) async-start(), calls=%async_computation.15 | async-start | bytes 18874368 | tf_op jit(solution)/shard_map/all_gather | solution.py:353
  643.5 593.9 %copy-start.21 = (bf16[256,8,128]{0,2,1:T(8,128)(2,1)S(1)}, bf16[256,8,128]{0,2,1:T(8,128)(2,1)}, u32[]{:S(2)}) copy-start(bf16[256,8,128]{0,2,1:T(8,128)(2,1)} %copy-done.20) | copy-start | bytes 1572868
  643.5 594.1 %copy-start.38 = (bf16[256,1024]{1,0:T(8,128)(2,1)S(1)}, bf16[256,1024]{1,0:T(8,128)(2,1)}, u32[]{:S(2)}) copy-start(bf16[256,1024]{1,0:T(8,128)(2,1)} %copy-done.37) | copy-start | bytes 1572868
  643.5 1071.3 %all-gather.35.cloned.1.call-start = ((), (), s32[]{:S(2)}) async-start(), calls=%async_computation.17 | async-start | bytes 1179648 | tf_op jit(solution)/shard_map/all_gather | solution.py:403
  764.3 953.2 %all-gather.37.cloned.1.call-start = ((), (), s32[]{:S(2)}) async-start(), calls=%async_computation.21 | async-start | bytes 1179648 | tf_op jit(solution)/shard_map/all_gather | solution.py:418
  916.5 803.9 %all-gather.39.cloned.1.call-start = ((), (), s32[]{:S(2)}) async-start(), calls=%async_computation.23 | async-start | bytes 1769472 | tf_op jit(solution)/shard_map/all_gather | solution.py:424
  1075.9 647.9 %all-gather.41.cloned.1.call-start = ((), (), s32[]{:S(2)}) async-start(), calls=%async_computation.25 | async-start | bytes 1769472 | tf_op jit(solution)/shard_map/all_gather | solution.py:427
  1237.3 490.0 %all-gather.43.cloned.1.call-start = ((), (), s32[]{:S(2)}) async-start(), calls=%async_computation.27 | async-start | bytes 1769472 | tf_op jit(solution)/shard_map/all_gather | solution.py:430
  1397.8 447.3 %reduce-scatter.10.cloned.1.call-start = ((), (), s32[]{:S(2)}) async-start(), calls=%async_computation.18 | async-start | bytes 4325376 | tf_op jit(solution)/shard_map/reduce_scatter | solution.py:389
  1548.4 149.0 %copy-start.35 = (f32[256,128]{0,1:T(8,128)S(1)}, f32[256,128]{0,1:T(8,128)}, u32[]{:S(2)}) copy-start(f32[256,128]{0,1:T(8,128)} %copy-done.33) | copy-start | bytes 393220
  1703.6 283.4 %reduce-scatter.12.cloned.1.call-start = ((), (), s32[]{:S(2)}) async-start(), calls=%async_computation.19 | async-start | bytes 4325376 | tf_op jit(solution)/shard_map/reduce_scatter | solution.py:390
  1707.8 2.5 copy-start.26
  1727.3 3.6 copy-start.15
  1727.3 3.6 copy-start.23
  1727.3 3.6 copy-start.45
  1732.5 60.3 %copy-start.64 = (f32[256]{0:T(256)S(1)}, f32[256]{0:T(256)}, u32[]{:S(2)}) copy-start(f32[256]{0:T(256)} %copy-done.63) | copy-start | bytes 3076
  1732.5 60.3 %copy-start.13 = (f32[256,1024]{1,0:T(8,128)S(1)}, f32[256,1024]{1,0:T(8,128)}, u32[]{:S(2)}) copy-start(f32[256,1024]{1,0:T(8,128)} %copy-done.11) | copy-start | bytes 3145732
  (40 other events, 54.5 us)
Sparse Core Ops, SparseCore 0:
  9.9 38.0 all-gather.16
  49.8 35.2 all-gather.18
  87.0 53.9 all-gather.22
  143.0 82.0 all-gather.20
  226.8 51.2 all-gather.24
  279.8 70.1 all-gather.26
  351.8 70.1 all-gather.28
  423.8 70.1 all-gather.30
  610.4 152.2 reduce-scatter.7
  764.8 149.9 reduce-scatter.13
  920.9 153.2 reduce-scatter.15
  1081.1 154.4 reduce-scatter.17
  1241.6 154.4 reduce-scatter.19
  1398.2 150.1 all-gather.32
  1550.5 20.2 all-gather.34
  1572.4 21.7 all-gather.36
  1596.3 24.6 all-gather.38
  1623.2 24.3 all-gather.40
  1649.3 24.5 all-gather.42
  1703.8 141.2 reduce-scatter.9
  1847.5 139.5 reduce-scatter.11
where the time goes:
time: 2020 us; the launch traced here: 2010 us
  waiting for transfers between devices  1330 us (66%)
  matrix products  258 us (13%)
  blocking collectives  165 us (8%)
  local copies, waits for them, and re-layouts  148 us (7%)
  other arithmetic  77.9 us (4%)
  between operations  20.9 us (1%)
    reduce_scatter x1, waiting for transfers between devices, per_device(): lax.psum_scatter(grads[9], ('fsdp', 'ctx'), scatter_dimension=0, tiled=True)  160 us
    reduce_scatter x1, waiting for transfers between devices, per_device(): lax.psum_scatter(grads[8], ('fsdp', 'ctx'), scatter_dimension=0, tiled=True)  158 us
    all_gather x1, waiting for transfers between devices, per_device(): lax.all_gather(query_pair, 'ctx', axis=0, tiled=True)  151 us
    reduce_scatter x1, waiting for transfers between devices, per_device(): lax.psum_scatter(grads[6], ('fsdp', 'ctx'), scatter_dimension=0, tiled=True)  150 us
    reduce_scatter x1, waiting for transfers between devices, per_device(): lax.psum_scatter(grads[10], ('fsdp', 'ctx'), scatter_dimension=0, tiled=T...  143 us
    reduce_scatter x1, waiting for transfers between devices, per_device(): lax.psum_scatter(grads[3], ('fsdp', 'ctx'), scatter_dimension=0, tiled=True)  125 us
    reduce_scatter x1, waiting for transfers between devices, per_device(): lax.psum_scatter(grads[1], ('fsdp', 'ctx'), scatter_dimension=0, tiled=True)  119 us
    psum x2, blocking collectives, per_device(): sq_total, count_total = lax.psum((sq_local, count_local), ('fsdp', 'ctx'))  79.1 us
  transfers between devices with their start and end apart: 21, of which 14 were waited for; matrix products, arithmetic and copies ran while one was open for 17% of the time, Pallas kernels for 0%

commit v1 on v0

--- a/solution.py
+++ b/solution.py
@@ -4,6 +4,8 @@
 import jax
 import jax.numpy as jnp
 from jax import lax
+from jax.experimental import pallas as pl
+from jax.experimental.pallas import tpu as pltpu
 from jax.sharding import PartitionSpec as P
 
 QUERY_HEADS = 16
@@ -449,9 +451,947 @@
     )
 
 
+MESH = pl.DeviceIdType.MESH
+BF16 = jnp.bfloat16
+F32 = jnp.float32
+GROUP = QUERY_HEADS // KEY_VALUE_HEADS
+HEAD_COLUMNS = (GROUP + 2) * HEAD_SIZE
+SCALE = 1.0 / math.sqrt(HEAD_SIZE)
+VMEM_LIMIT = 56 * 1024 * 1024
+
+
+class Place:
+    def __init__(self):
+        self.f = lax.axis_index("fsdp")
+        self.c = lax.axis_index("ctx")
+        self.z = self.c // 2
+        self.k = self.c % 2
+        self.fx = self.f + 1 - 2 * (self.f % 2)
+        self.fy = (self.f + 2) % 4
+        self.fd = 3 - self.f
+        self.xp = (self.fx, self.c)
+        self.yp = (self.fy, self.c)
+        self.dp = (self.fd, self.c)
+        self.sib = (self.f, self.c + 1 - 2 * self.k)
+
+    def along_z(self, step):
+        other = (self.z + step) % 4
+        return other, (self.f, 2 * other + self.k)
+
+    def along_ctx(self, step):
+        other = (self.c + step) % 8
+        return other, (self.f, other)
+
+
+def greet(partners):
+    barrier = pltpu.get_barrier_semaphore()
+    for partner in partners:
+        pl.semaphore_signal(barrier, inc=1, device_id=partner, device_id_type=MESH)
+    pl.semaphore_wait(barrier, len(partners))
+
+
+class Copies:
+    def __init__(self, send, recv):
+        self.send, self.recv, self.used = send, recv, 0
+
+    def take(self, count):
+        first = self.used
+        self.used += count
+        return first
+
+    def at(self, index, src, dst, partner):
+        return pltpu.make_async_remote_copy(
+            src_ref=src,
+            dst_ref=dst,
+            send_sem=self.send.at[index],
+            recv_sem=self.recv.at[index],
+            device_id=partner,
+            device_id_type=MESH,
+        )
+
+    def __call__(self, src, dst, partner):
+        return self.at(self.take(1), src, dst, partner)
+
+
+class Locals:
+    def __init__(self, sems):
+        self.sems, self.used, self.open = sems, 0, []
+
+    def __call__(self, src, dst):
+        copy = pltpu.make_async_copy(src, dst, self.sems.at[self.used])
+        self.used += 1
+        copy.start()
+        self.open.append(copy)
+        return copy
+
+    def wait(self):
+        for copy in self.open:
+            copy.wait()
+        self.open = []
+
+
+def add_rows(dst, sources):
+    rows = dst.shape[0]
+    step = 32
+
+    @pl.loop(0, rows // step)
+    def _(i):
+        part = pl.ds(pl.multiple_of(i * step, step), step)
+        total = sources[0][part, :].astype(F32)
+        for source in sources[1:]:
+            total = total + source[part, :].astype(F32)
+        dst[part, :] = total.astype(dst.dtype)
+
+
+class Gather:
+    def __init__(self, me, copies, buf):
+        half = buf.shape[1] // 2
+        a, b = pl.ds(0, half), pl.ds(half, half)
+        own_a, own_b = buf.at[me.f, a], buf.at[me.f, b]
+        self.a_x = copies(own_a, own_a, me.xp)
+        self.b_y = copies(own_b, own_b, me.yp)
+        self.b_x = copies(own_b, own_b, me.xp)
+        self.a_y = copies(own_a, own_a, me.yp)
+        self.on_y = copies(buf.at[me.fx, a], buf.at[me.fx, a], me.yp)
+        self.on_x = copies(buf.at[me.fy, b], buf.at[me.fy, b], me.xp)
+
+    def first(self):
+        self.a_x.start()
+        self.b_y.start()
+
+    def second(self):
+        self.b_x.start()
+        self.a_y.start()
+
+    def relay(self):
+        self.a_x.wait_recv()
+        self.on_y.start()
+        self.b_y.wait_recv()
+        self.on_x.start()
+
+    def finish(self):
+        for copy in (self.b_x, self.a_y, self.on_y, self.on_x):
+            copy.wait_recv()
+        for copy in (self.a_x, self.b_y, self.b_x, self.a_y, self.on_y, self.on_x):
+            copy.wait_send()
+
+
+def scatter_buffers(rows, columns):
+    half = rows // 2
+    return [pltpu.VMEM((12, half, columns), BF16)]
+
+
+class Scatter:
+    def __init__(self, me, copies, local, part, bufs):
+        half = part.shape[1] // 2
+        a, b = pl.ds(0, half), pl.ds(half, half)
+        slot = [bufs.at[i] for i in range(12)]
+        self.fwd_a, self.fwd_b, self.own_a, self.own_b = slot[0:4]
+        self.rx_own, self.rx_fwd, self.ry_own, self.ry_fwd, self.r2_a, self.r2_b = slot[4:10]
+        self.sum_a, self.sum_b = slot[10:12]
+        self.d_x = copies(part.at[me.fd, a], self.rx_fwd, me.xp)
+        self.d_y = copies(part.at[me.fd, b], self.ry_fwd, me.yp)
+        self.o_x = copies(part.at[me.fx, a], self.rx_own, me.xp)
+        self.o_y = copies(part.at[me.fy, b], self.ry_own, me.yp)
+        self.to_y = copies(self.fwd_a, self.r2_a, me.yp)
+        self.to_x = copies(self.fwd_b, self.r2_b, me.xp)
+        self.local, self.me, self.part, self.a, self.b = local, me, part, a, b
+
+    def first(self):
+        self.d_x.start()
+        self.d_y.start()
+
+    def second(self):
+        self.o_x.start()
+        self.o_y.start()
+        me, part = self.me, self.part
+        self.mine = [
+            self.local(part.at[me.fy, self.a], self.fwd_a),
+            self.local(part.at[me.fx, self.b], self.fwd_b),
+            self.local(part.at[me.f, self.a], self.own_a),
+            self.local(part.at[me.f, self.b], self.own_b),
+        ]
+
+    def relay(self):
+        for copy in self.mine:
+            copy.wait()
+        self.d_x.wait_recv()
+        add_rows(self.fwd_a, [self.fwd_a, self.rx_fwd])
+        self.to_y.start()
+        self.d_y.wait_recv()
+        add_rows(self.fwd_b, [self.fwd_b, self.ry_fwd])
+        self.to_x.start()
+
+    def finish(self, sum_a, sum_b):
+        self.o_x.wait_recv()
+        self.to_y.wait_recv()
+        add_rows(sum_a, [self.own_a, self.rx_own, self.r2_a])
+        self.o_y.wait_recv()
+        self.to_x.wait_recv()
+        add_rows(sum_b, [self.own_b, self.ry_own, self.r2_b])
+
+    def drain(self):
+        for copy in (self.d_x, self.d_y, self.o_x, self.o_y, self.to_y, self.to_x):
+            copy.wait_send()
+
+
+class LineSum:
+    def __init__(self, me, copies, own, bufs):
+        z, f, k = me.z, me.f, me.k
+        self.inner = (z == 1) | (z == 2)
+        self.outer = (z == 0) | (z == 3)
+        self.mine = z - 1
+        self.theirs = 2 - z
+        self.own, self.from_outer, self.total, self.from_inner = own, bufs.at[0:2], bufs.at[2:4], bufs.at[4]
+        self.copies = copies
+        self.base = copies.take(8)
+        self.inner_of = (f, 2 * (1 + z // 3) + k)
+        self.outer_of = (f, 2 * (3 * (z - 1)) + k)
+        self.partner = (f, 2 * (3 - z) + k)
+
+    def inward(self, half):
+        return self.copies.at(
+            self.base + half, self.own.at[half], self.from_outer.at[half], self.inner_of
+        )
+
+    def across(self, half):
+        return self.copies.at(
+            self.base + 2 + half, self.own.at[half], self.from_inner, self.partner
+        )
+
+    def back_across(self, half):
+        return self.copies.at(
+            self.base + 4 + half, self.total.at[half], self.total.at[half], self.partner
+        )
+
+    def outward(self, half):
+        return self.copies.at(
+            self.base + 6 + half, self.total.at[half], self.total.at[half], self.outer_of
+        )
+
+    def start(self):
+        @pl.when(self.outer)
+        def _():
+            self.inward(0).start()
+            self.inward(1).start()
+
+    def meet(self):
+        @pl.when(self.inner)
+        def _():
+            t, m = self.theirs, self.mine
+            self.inward(t).wait_recv()
+            add_rows(self.own.at[t], [self.own.at[t], self.from_outer.at[t]])
+            self.across(t).start()
+
+    def close(self):
+        @pl.when(self.inner)
+        def _():
+            m = self.mine
+            self.inward(m).wait_recv()
+            self.across(m).wait_recv()
+            add_rows(
+                self.total.at[m], [self.own.at[m], self.from_outer.at[m], self.from_inner]
+            )
+            self.back_across(m).start()
+            self.outward(m).start()
+
+    def spread(self):
+        @pl.when(self.inner)
+        def _():
+            t = self.theirs
+            self.back_across(t).wait_recv()
+            self.outward(t).start()
+
+    def arrive(self):
+        @pl.when(self.outer)
+        def _():
+            self.outward(0).wait_recv()
+            self.outward(1).wait_recv()
+
+    def drain(self):
+        @pl.when(self.outer)
+        def _():
+            self.inward(0).wait_send()
+            self.inward(1).wait_send()
+
+        @pl.when(self.inner)
+        def _():
+            self.across(self.theirs).wait_send()
+            self.back_across(self.mine).wait_send()
+            self.outward(0).wait_send()
+            self.outward(1).wait_send()
+
+
+class SmallSum:
+    def __init__(self, me, copies, own, plane, line):
+        self.me, self.own, self.plane, self.line = me, own, plane, line
+        f = me.f
+        self.step_one = [
+            copies(own, plane.at[f], partner) for partner in (me.xp, me.yp, me.dp)
+        ]
+        self.step_two = [
+            copies(line.at[me.c], line.at[me.c], me.along_ctx(step)[1]) for step in range(1, 8)
+        ]
+
+    def first(self):
+        for copy in self.step_one:
+            copy.start()
+        self.plane[self.me.f] = self.own[...]
+
+    def second(self):
+        for copy in self.step_one:
+            copy.wait_recv()
+        plane = self.plane
+        self.line[self.me.c] = (plane[0] + plane[1]) + (plane[2] + plane[3])
+        for copy in self.step_two:
+            copy.start()
+
+    def finish(self, dst):
+        for copy in self.step_two:
+            copy.wait_recv()
+        line = self.line
+        total = line[0]
+        for i in range(1, 8):
+            total = total + line[i]
+        dst[...] = total
+
+    def drain(self):
+        for copy in self.step_one + self.step_two:
+            copy.wait_send()
+
+
+HBM = pl.BlockSpec(memory_space=pl.ANY)
+VM = pl.BlockSpec(memory_space=pltpu.VMEM)
+
+
+def transfer(kernel, name, number, args, in_specs, outs, out_specs, scratch, copies, local):
+    return pl.pallas_call(
+        kernel,
+        out_shape=outs,
+        in_specs=in_specs,
+        out_specs=out_specs,
+        scratch_shapes=scratch
+        + [
+            pltpu.SemaphoreType.DMA((copies,)),
+            pltpu.SemaphoreType.DMA((copies,)),
+            pltpu.SemaphoreType.DMA((local,)),
+        ],
+        compiler_params=pltpu.CompilerParams(
+            collective_id=number, has_side_effects=True, vmem_limit_bytes=VMEM_LIMIT
+        ),
+        name=name,
+    )(*args)
+
+
+def shape(dims, dtype):
+    return jax.ShapeDtypeStruct(dims, dtype)
+
+
+def kernel_begin(
+    wq, wk, wv, x, t, misc, gains, count,
+    w_all, x_pair, t_pair, misc_pair, gains_all, count_out,
+    plane, line, send, recv, lsem,
+):
+    me = Place()
+    ctx = [me.along_ctx(step)[1] for step in range(1, 8)]
+    greet([me.xp, me.yp, me.dp] + ctx)
+    copies, local = Copies(send, recv), Locals(lsem)
+    q = GROUP * HEAD_SIZE
+    for i in range(KEY_VALUE_HEADS // 2):
+        head = 2 * i + me.k
+        at = HEAD_COLUMNS * i
+        q_at = pl.ds(pl.multiple_of(head * q, HEAD_SIZE), q)
+        k_at = pl.ds(pl.multiple_of(head * HEAD_SIZE, HEAD_SIZE), HEAD_SIZE)
+        local(wq.at[:, q_at], w_all.at[me.f, :, pl.ds(at, q)])
+        local(wk.at[:, k_at], w_all.at[me.f, :, pl.ds(at + q, HEAD_SIZE)])
+        local(wv.at[:, k_at], w_all.at[me.f, :, pl.ds(at + q + HEAD_SIZE, HEAD_SIZE)])
+    small = SmallSum(me, copies, count, plane, line)
+    small.first()
+    others = [copies(gains, gains_all.at[me.f], partner) for partner in (me.xp, me.yp, me.dp)]
+    for src, dst in ((x, x_pair), (t, t_pair), (misc, misc_pair)):
+        others.append(copies(src, dst.at[me.k], me.sib))
+    for copy in others:
+        copy.start()
+    local.wait()
+    weights = Gather(me, copies, w_all)
+    weights.first()
+    weights.second()
+    for src, dst in ((x, x_pair), (t, t_pair), (misc, misc_pair)):
+        local(src, dst.at[me.k])
+    local(gains, gains_all.at[me.f])
+    small.second()
+    weights.relay()
+    local.wait()
+    small.finish(count_out)
+    for copy in others:
+        copy.wait_recv()
+    weights.finish()
+    for copy in others:
+        copy.wait_send()
+    small.drain()
+
+
+def begin(wq, wk, wv, x, t, misc, gains, count):
+    rows = wq.shape[0]
+    columns = (KEY_VALUE_HEADS // 2) * HEAD_COLUMNS
+    return transfer(
+        kernel_begin, "begin", 1,
+        (wq, wk, wv, x, t, misc, gains, count),
+        [HBM] * 7 + [VM],
+        [
+            shape((4, rows, columns), BF16),
+            shape((2,) + x.shape, BF16),
+            shape((2,) + t.shape, BF16),
+            shape((2, 8, 128), F32),
+            shape((4, 8, 128), F32),
+            shape((8, 128), F32),
+        ],
+        [HBM] * 5 + [VM],
+        [pltpu.VMEM((4, 8, 128), F32), pltpu.VMEM((8, 8, 128), F32)],
+        24, 20,
+    )
+
+
+class Exchange:
+    def __init__(self, me, copies, local, piece, place):
+        self.me, self.local, self.piece, self.place = me, local, piece, place
+        self.sends = []
+        for step in (2, 1, 3):
+            other, partner = me.along_z(step)
+            self.sends.append(copies(piece(other), place(me.z), partner))
+
+    def start(self):
+        for copy in self.sends:
+            copy.start()
+        self.own = self.local(self.piece(self.me.z), self.place(self.me.z))
+
+    def finish(self):
+        self.own.wait()
+        for copy in self.sends:
+            copy.wait()
+
+
+def kernel_to_heads(qkv, wg, wu, qkv_all, wg_all, wu_all, send, recv, lsem):
+    me = Place()
+    greet([me.xp, me.yp] + [me.along_z(step)[1] for step in (1, 2, 3)])
+    copies, local, second = Copies(send, recv), Locals(lsem), Locals(lsem)
+    move = Exchange(
+        me, copies, local, lambda z: qkv.at[z], lambda z: qkv_all.at[z]
+    )
+    move.start()
+    second.used = 1
+    width = wg.shape[1] // 8
+    for src, dst in ((wg, wg_all), (wu, wu_all)):
+        for i in range(4):
+            at = pl.ds(pl.multiple_of((2 * i + me.k) * width, 128), width)
+            second(src.at[:, at], dst.at[me.f, :, pl.ds(i * width, width)])
+    second.wait()
+    gathers = [Gather(me, copies, wg_all), Gather(me, copies, wu_all)]
+    for gather in gathers:
+        gather.first()
+    for gather in gathers:
+        gather.second()
+    for gather in gathers:
+        gather.relay()
+    move.finish()
+    for gather in gathers:
+        gather.finish()
+
+
+def to_heads(qkv, wg, wu):
+    rows, columns = wg.shape
+    return transfer(
+        kernel_to_heads, "to_heads", 2,
+        (qkv, wg, wu), [HBM] * 3,
+        [
+            shape(qkv.shape, BF16),
+            shape((4, rows, columns // 2), BF16),
+            shape((4, rows, columns // 2), BF16),
+        ],
+        [HBM] * 3, [], 15, 9,
+    )
+
+
+def kernel_to_tokens(att, wd, wo, att_all, wd_all, wo_all, send, recv, lsem):
+    me = Place()
+    greet([me.xp, me.yp] + [me.along_z(step)[1] for step in (1, 2, 3)])
+    copies, local, second = Copies(send, recv), Locals(lsem), Locals(lsem)
+    tokens, width = att_all.shape[0], att.shape[1]
+    second.used = 1
+    for src, dst in ((wd, wd_all), (wo, wo_all)):
+        rows = dst.shape[1]
+        second(src.at[pl.ds(pl.multiple_of(me.k * rows, 16), rows)], dst.at[me.f])
+    move = Exchange(
+        me, copies, local,
+        lambda z: att.at[pl.ds(pl.multiple_of(z * tokens, 16), tokens)],
+        lambda z: att_all.at[:, pl.ds(pl.multiple_of(z * width, 128), width)],
+    )
+    move.start()
+    second.wait()
+    gathers = [Gather(me, copies, wo_all), Gather(me, copies, wd_all)]
+    for gather in gathers:
+        gather.first()
+    for gather in gathers:
+        gather.second()
+    for gather in gathers:
+        gather.relay()
+    move.finish()
+    for gather in gathers:
+        gather.finish()
+
+
+def to_tokens(att, wd, wo):
+    return transfer(
+        kernel_to_tokens, "to_tokens", 3,
+        (att, wd, wo), [HBM] * 3,
+        [
+            shape((att.shape[0] // 4, att.shape[1] * 4), BF16),
+            shape((4, wd.shape[0] // 2, wd.shape[1]), BF16),
+            shape((4, wo.shape[0] // 2, wo.shape[1]), BF16),
+        ],
+        [HBM] * 3, [], 15, 3,
+    )
+
+
+def kernel_swap(src, dst, send, recv, lsem):
+    me = Place()
+    greet([me.sib])
+    copy = Copies(send, recv)(src, dst, me.sib)
+    copy.start()
+    copy.wait()
+
+
+def swap(value, number):
+    return transfer(
+        kernel_swap, "swap%d" % number, number, (value,), [HBM], shape(value.shape, value.dtype), HBM, [], 1, 1
+    )
+
+
+def run_scatters(me, copies, local, move, scatters, outs):
+    move.start()
+    for scatter in scatters:
+        scatter.first()
+    for scatter in scatters:
+        scatter.second()
+    for scatter in scatters:
+        scatter.relay()
+    writes = []
+    for scatter, out in zip(scatters, outs):
+        scatter.finish(scatter.sum_a, scatter.sum_b)
+        half = out.shape[0] // 2
+        writes.append(local(scatter.sum_a, out.at[pl.ds(0, half)]))
+        writes.append(local(scatter.sum_b, out.at[pl.ds(half, half)]))
+    move.finish()
+    for scatter in scatters:
+        scatter.drain()
+    for write in writes:
+        write.wait()
+
+
+def kernel_grads_to_heads(grads, down, grads_all, down_sum, bufs, send, recv, lsem):
+    me = Place()
+    greet([me.xp, me.yp] + [me.along_z(step)[1] for step in (1, 2, 3)])
+    copies, local = Copies(send, recv), Locals(lsem)
+    width = grads_all.shape[2]
+    move = Exchange(
+        me, copies, local,
+        lambda z: grads.at[:, pl.ds(pl.multiple_of(z * width, 128), width)],
+        lambda z: grads_all.at[z],
+    )
+    run_scatters(me, copies, local, move, [Scatter(me, copies, local, down, bufs)], [down_sum])
+
+
+def grads_to_heads(grads, down):
+    tokens, columns = grads.shape
+    return transfer(
+        kernel_grads_to_heads, "grads_to_heads", 4,
+        (grads, down), [HBM] * 2,
+        [shape((4, tokens, columns // 4), BF16), shape(down.shape[1:], BF16)],
+        [HBM] * 2, scatter_buffers(*down.shape[1:]), 9, 7,
+    )
+
+
+def kernel_grads_to_tokens(grads, gate, up, grads_all, gate_sum, up_sum, bufs_g, bufs_u, send, recv, lsem):
+    me = Place()
+    greet([me.xp, me.yp] + [me.along_z(step)[1] for step in (1, 2, 3)])
+    copies, local = Copies(send, recv), Locals(lsem)
+    tokens, width = grads_all.shape[0], grads.shape[1]
+    move = Exchange(
+        me, copies, local,
+        lambda z: grads.at[pl.ds(pl.multiple_of(z * tokens, 16), tokens)],
+        lambda z: grads_all.at[:, pl.ds(pl.multiple_of(z * width, 128), width)],
+    )
+    run_scatters(
+        me, copies, local, move,
+        [Scatter(me, copies, local, gate, bufs_g), Scatter(me, copies, local, up, bufs_u)],
+        [gate_sum, up_sum],
+    )
+
+
+def grads_to_tokens(grads, gate, up):
+    return transfer(
+        kernel_grads_to_tokens, "grads_to_tokens", 5,
+        (grads, gate, up), [HBM] * 3,
+        [
+            shape((grads.shape[0] // 4, grads.shape[1] * 4), BF16),
+            shape(gate.shape[1:], BF16),
+            shape(up.shape[1:], BF16),
+        ],
+        [HBM] * 3,
+        scatter_buffers(*gate.shape[1:]) + scatter_buffers(*up.shape[1:]), 15, 13,
+    )
+
+
+def kernel_end(
+    down, gate, up, out, qkv, small,
+    down_tot, gate_tot, up_tot, out_tot, qkv_tot, small_tot,
+    own_d, own_g, own_u, own_o, own_q, line_d, line_g, line_u, line_o, line_q, sc_o, sc_q, plane, line,
+    send, recv, lsem,
+):
+    me = Place()
+    greet([me.xp, me.yp, me.dp] + [me.along_ctx(step)[1] for step in range(1, 8)])
+    copies, local = Copies(send, recv), Locals(lsem)
+    total = SmallSum(me, copies, small, plane, line)
+    total.first()
+    loads = []
+    for src, own in ((down, own_d), (gate, own_g), (up, own_u)):
+        half = own.shape[1]
+        loads.append(
+            [local(src.at[pl.ds(i * half, half)], own.at[i]) for i in range(2)]
+        )
+    scatters = [Scatter(me, copies, local, out, sc_o), Scatter(me, copies, local, qkv, sc_q)]
+    for scatter in scatters:
+        scatter.first()
+    for scatter in scatters:
+        scatter.second()
+    total.second()
+    sums = [
+        LineSum(me, copies, own, bufs)
+        for own, bufs in (
+            (own_d, line_d), (own_g, line_g), (own_u, line_u), (own_o, line_o), (own_q, line_q)
+        )
+    ]
+    totals = (down_tot, gate_tot, up_tot, out_tot, qkv_tot)
+    for load, entry in zip(loads, sums):
+        for copy in load:
+            copy.wait()
+        entry.start()
+    base = copies.take(len(sums) * 2)
+    swaps, writes = [], []
+
+    def finish(i):
+        sums[i].spread()
+        sums[i].arrive()
+        half = sums[i].total.shape[1]
+        for j in range(2):
+            dst = totals[i].at[me.k, pl.ds(j * half, half)]
+            copy = copies.at(base + 2 * i + j, sums[i].total.at[j], dst, me.sib)
+            copy.start()
+            swaps.append(copy)
+            writes.append(local(sums[i].total.at[j], dst))
+
+    sums[0].meet()
+    scatters[0].relay()
+    sums[0].close()
+    sums[1].meet()
+    scatters[1].relay()
+    scatters[0].finish(own_o.at[0], own_o.at[1])
+    sums[3].start()
+    sums[1].close()
+    sums[2].meet()
+    finish(0)
+    scatters[1].finish(own_q.at[0], own_q.at[1])
+    sums[4].start()
+    sums[2].close()
+    sums[3].meet()
+    finish(1)
+    sums[3].close()
+    sums[4].meet()
+    finish(2)
+    sums[4].close()
+    finish(3)
+    finish(4)
+    total.finish(small_tot)
+    total.drain()
+    for scatter in scatters:
+        scatter.drain()
+    for entry in sums:
+        entry.drain()
+    for copy in swaps:
+        copy.wait()
+    for copy in writes:
+        copy.wait()
+
+
+def end(down, gate, up, out, qkv, small):
+    sizes = [down.shape, gate.shape, up.shape, out.shape[1:], qkv.shape[1:]]
+    own = [pltpu.VMEM((2, r // 2, c), BF16) for r, c in sizes]
+    line = [pltpu.VMEM((5, r // 2, c), BF16) for r, c in sizes]
+    return transfer(
+        kernel_end, "end", 6,
+        (down, gate, up, out, qkv, small), [HBM] * 5 + [VM],
+        [shape((2,) + tuple(s), BF16) for s in sizes] + [shape(small.shape, F32)],
+        [HBM] * 5 + [VM],
+        own + line
+        + scatter_buffers(*out.shape[1:])
+        + scatter_buffers(*qkv.shape[1:])
+        + [pltpu.VMEM((4,) + small.shape, F32), pltpu.VMEM((8,) + small.shape, F32)],
+        10 + 12 + 5 * 8 + 10, 6 + 8 + 10,
+    )
+
+
+def dot_nt(a, b, **kw):
+    return lax.dot_general(a, b, (((1,), (1,)), ((), ())), preferred_element_type=F32, **kw)
+
+
+def dot_nn(a, b):
+    return lax.dot_general(a, b, (((1,), (0,)), ((), ())), preferred_element_type=F32)
+
+
+def dot_tn(a, b):
+    return lax.dot_general(a, b, (((0,), (0,)), ((), ())), preferred_element_type=F32)
+
+
+BLOCK = 512
+HIGHEST = lax.Precision.HIGHEST
+
+
+def attend_kernel(qkv, att, lse, values):
+    blocks = qkv.shape[0] // BLOCK
+    k_at = pl.ds(GROUP * HEAD_SIZE, HEAD_SIZE)
+    values[:, 0:HEAD_SIZE] = qkv[:, (GROUP + 1) * HEAD_SIZE :]
+    values[:, HEAD_SIZE:] = jnp.ones((qkv.shape[0], HEAD_SIZE), BF16)
+    row = lax.broadcasted_iota(jnp.int32, (BLOCK, BLOCK), 0)
+    column = lax.broadcasted_iota(jnp.int32, (BLOCK, BLOCK), 1)
+    allowed = column <= row
+
+    @pl.loop(0, blocks)
+    def _(i):
+        rows = pl.ds(pl.multiple_of(i * BLOCK, BLOCK), BLOCK)
+        for g in range(GROUP):
+            q = qkv[rows, pl.ds(g * HEAD_SIZE, HEAD_SIZE)]
+
+            def part(j, acc, q=q):
+                keys = pl.ds(pl.multiple_of(j * BLOCK, BLOCK), BLOCK)
+                e = jnp.exp(dot_nt(q, qkv[keys, k_at]) * SCALE)
+                return acc + dot_nn(e.astype(BF16), values[keys, :])
+
+            acc = lax.fori_loop(0, i, part, jnp.zeros((BLOCK, 2 * HEAD_SIZE), F32))
+            e = jnp.exp(dot_nt(q, qkv[rows, k_at]) * SCALE)
+            acc = acc + dot_nn(jnp.where(allowed, e, 0.0).astype(BF16), values[rows, :])
+            total = acc[:, HEAD_SIZE:]
+            att[rows, pl.ds(g * HEAD_SIZE, HEAD_SIZE)] = (acc[:, :HEAD_SIZE] / total).astype(BF16)
+            mean = jnp.full((8, HEAD_SIZE), 1.0 / HEAD_SIZE, F32)
+            lse[g, :, rows] = dot_nt(mean, jnp.log(total), precision=HIGHEST)
+
+
+def attend(qkv):
+    tokens = qkv.shape[0]
+    return pl.pallas_call(
+        attend_kernel,
+        out_shape=[shape((tokens, GROUP * HEAD_SIZE), BF16), shape((GROUP, 8, tokens), F32)],
+        in_specs=[VM],
+        out_specs=[VM, VM],
+        scratch_shapes=[pltpu.VMEM((tokens, 2 * HEAD_SIZE), BF16)],
+        compiler_params=pltpu.CompilerParams(vmem_limit_bytes=VMEM_LIMIT),
+        name="attend",
+    )(qkv)
+
+
+def attend_back_kernel(qkv, att, g_out, lse, grads, g_k, g_v):
+    blocks = qkv.shape[0] // BLOCK
+    k_at = pl.ds(GROUP * HEAD_SIZE, HEAD_SIZE)
+    v_at = pl.ds((GROUP + 1) * HEAD_SIZE, HEAD_SIZE)
+    g_k[...] = jnp.zeros_like(g_k)
+    g_v[...] = jnp.zeros_like(g_v)
+    key = lax.broadcasted_iota(jnp.int32, (BLOCK, BLOCK), 0)
+    query = lax.broadcasted_iota(jnp.int32, (BLOCK, BLOCK), 1)
+    allowed = key <= query
+
+    @pl.loop(0, blocks)
+    def _(i):
+        rows = pl.ds(pl.multiple_of(i * BLOCK, BLOCK), BLOCK)
+        for g in range(GROUP):
+            head = pl.ds(g * HEAD_SIZE, HEAD_SIZE)
+            q = qkv[rows, head]
+            go = g_out[rows, head]
+            product = go.astype(F32) * att[rows, head].astype(F32)
+            delta = dot_nt(jnp.ones((8, HEAD_SIZE), F32), product, precision=HIGHEST)[0:1, :]
+            log_sum = lse[g, 0:1, rows]
+
+            def part(keys, masked, q=q, go=go, delta=delta, log_sum=log_sum):
+                k, v = qkv[keys, k_at], qkv[keys, v_at]
+                p = jnp.exp(dot_nt(k, q) * SCALE - log_sum)
+                if masked:
+                    p = jnp.where(allowed, p, 0.0)
+                gs = (p * (dot_nt(v, go) - delta) * SCALE).astype(BF16)
+                g_v[keys, :] += dot_nn(p.astype(BF16), go)
+                g_k[keys, :] += dot_nn(gs, q)
+                return dot_tn(gs, k)
+
+            def step(j, acc, part=part):
+                return acc + part(pl.ds(pl.multiple_of(j * BLOCK, BLOCK), BLOCK), False)
+
+            acc = lax.fori_loop(0, i, step, jnp.zeros((BLOCK, HEAD_SIZE), F32))
+            grads[rows, head] = (acc + part(rows, True)).astype(BF16)
+
+    grads[:, k_at] = g_k[...].astype(BF16)
+    grads[:, v_at] = g_v[...].astype(BF16)
+
+
+def attend_back(qkv, att, g_out, lse):
+    tokens = qkv.shape[0]
+    return pl.pallas_call(
+        attend_back_kernel,
+        out_shape=shape(qkv.shape, BF16),
+        in_specs=[VM] * 4,
+        out_specs=VM,
+        scratch_shapes=[pltpu.VMEM((tokens, HEAD_SIZE), F32)] * 2,
+        compiler_params=pltpu.CompilerParams(vmem_limit_bytes=VMEM_LIMIT),
+        name="attend_back",
+    )(qkv, att, g_out, lse)
+
+
+def turn(values, cosine_table, sine_table):
+    half_width = HEAD_SIZE // 2
+    swapped = jnp.concatenate([values[..., half_width:], values[..., :half_width]], -1)
+    return values * cosine_table + swapped * sine_table
+
+
+def heads_of(cosine_table, sine_table, projected, gain_q, gain_k):
+    gain = jnp.concatenate([jnp.broadcast_to(gain_q, (GROUP, HEAD_SIZE)), gain_k[None]], 0)
+    first = root_mean_norm(projected[:, :, : GROUP + 1], gain)
+    first = turn(first, cosine_table[:, None, None, :], sine_table[:, None, None, :])
+    return jnp.concatenate([first, projected[:, :, GROUP + 1 :]], 2)
+
+
+def chip_step(
+    hidden_in, teacher, valid, positions, norm_attn, w_query, key_projection, value_projection,
+    gain_query, gain_key, w_out, norm_mlp, w_gate, w_up, w_down,
+):
+    f, c = lax.axis_index("fsdp"), lax.axis_index("ctx")
+    k = c % 2
+    rows = hidden_in.shape[1]
+    tokens = 2 * rows
+    width = hidden_in.shape[2]
+    heads = KEY_VALUE_HEADS // 2
+    misc = jnp.concatenate(
+        [positions.reshape(-1, 128), valid.reshape(-1, 128), jnp.zeros((4, 128), jnp.int32)], 0
+    ).astype(F32)
+    gains = jnp.concatenate(
+        [norm_attn, norm_mlp, gain_query, gain_key, jnp.zeros((448,), BF16)]
+    ).astype(F32).reshape(8, 128)
+    count = jnp.full((8, 128), jnp.sum(valid).astype(F32))
+    w_qkv, x_pair, t_pair, misc_pair, gains_all, count = begin(
+        w_query, key_projection, value_projection, hidden_in[0], teacher[0], misc, gains, count
+    )
+    w_qkv = w_qkv.reshape(width, -1)
+    count_total = count[0, 0]
+    x = x_pair.reshape(tokens, width).astype(F32)
+    target = t_pair.reshape(tokens, width).astype(F32)
+    token_positions = misc_pair[:, 0:2].reshape(tokens)
+    weight_rows = misc_pair[:, 2:4].reshape(tokens)
+    gain_one = gains_all[:, 0:2].reshape(width)
+    gain_two = gains_all[:, 2:4].reshape(width)
+    gain_q = gains_all[:, 4, 0:32].reshape(HEAD_SIZE)
+    gain_k = gains_all[:, 4, 32:64].reshape(HEAD_SIZE)
+
+    normed_one, norm_one_back = jax.vjp(root_mean_norm, x, gain_one)
+    hidden_one = normed_one.astype(BF16)
+    projected = jnp.dot(hidden_one, w_qkv, preferred_element_type=F32)
+    cosine_table, sine_table = rope_tables(token_positions)
+    qkv, heads_back = jax.vjp(
+        partial(heads_of, cosine_table, sine_table),
+        projected.reshape(tokens, heads, GROUP + 2, HEAD_SIZE), gain_q, gain_k,
+    )
+    qkv = qkv.astype(BF16).reshape(tokens, heads, HEAD_COLUMNS).transpose(1, 0, 2)
+    qkv_all, wg, wu = to_heads(qkv, w_gate, w_up)
+    qkv_all = qkv_all.reshape(4 * tokens, HEAD_COLUMNS)
+    wg, wu = wg.reshape(width, -1), wu.reshape(width, -1)
+    att, lse = attend(qkv_all)
+    att_all, wd, wo = to_tokens(att, w_down, w_out)
+    wd, wo = wd.reshape(-1, width), wo.reshape(-1, width)
+
+    def over_cores(part, number):
+        part = part.astype(BF16)
+        return part.astype(F32) + swap(part, number).astype(F32)
+
+    x2 = x + over_cores(jnp.dot(att_all, wo, preferred_element_type=F32), 7)
+    normed_two, norm_two_back = jax.vjp(root_mean_norm, x2, gain_two)
+    hidden_two = normed_two.astype(BF16)
+    gate = jnp.dot(hidden_two, wg, preferred_element_type=F32)
+    up = jnp.dot(hidden_two, wu, preferred_element_type=F32)
+    gated, gated_back = jax.vjp(swiglu, gate, up)
+    mid = gated.astype(BF16)
+    fin = x2 + over_cores(jnp.dot(mid, wd, preferred_element_type=F32), 8)
+    mismatch = fin - target
+    sq_local = 0.5 * jnp.sum(weight_rows[:, None] * mismatch * mismatch)
+    loss_scale = tokens // 2 * lax.axis_size("ctx") * lax.axis_size("fsdp") / 4.0
+    g_fin = 2.0 * loss_scale / count_total * weight_rows[:, None] * mismatch
+    g_dn = g_fin.astype(BF16)
+    g_gate, g_up = gated_back(against(g_dn, wd))
+    g_gate, g_up = g_gate.astype(BF16), g_up.astype(BF16)
+    g_h2 = over_cores(against(g_gate, wg) + against(g_up, wu), 9)
+    g_norm, grad_norm_mlp = norm_two_back(g_h2)
+    g_x2 = g_fin + g_norm
+    g_a = g_x2.astype(BF16)
+    g_o = against(g_a, wo).astype(BF16)
+    p_down = contract_rows(mid, g_dn).astype(BF16).reshape(4, -1, width)
+    g_o_all, s_down = grads_to_heads(g_o, p_down)
+    p_gate = contract_rows(hidden_two, g_gate).astype(BF16).reshape(4, width // 4, -1)
+    p_up = contract_rows(hidden_two, g_up).astype(BF16).reshape(4, width // 4, -1)
+    p_out = contract_rows(att_all, g_a).astype(BF16).reshape(4, -1, width)
+    g_qkv = attend_back(qkv_all, att, g_o_all.reshape(4 * tokens, -1), lse)
+    g_qkv_all, s_gate, s_up = grads_to_tokens(g_qkv, p_gate, p_up)
+    g_proj, grad_gain_q, grad_gain_k = heads_back(
+        g_qkv_all.reshape(tokens, heads, GROUP + 2, HEAD_SIZE).astype(F32)
+    )
+    g_proj = g_proj.astype(BF16).reshape(tokens, -1)
+    p_qkv = contract_rows(hidden_one, g_proj).astype(BF16).reshape(4, width // 4, -1)
+    g_h1 = over_cores(against(g_proj, w_qkv), 10)
+    g_norm, grad_norm_attn = norm_one_back(g_h1)
+    grad_input = lax.dynamic_slice_in_dim(g_x2 + g_norm, k * rows, rows, 0)
+    small = jnp.concatenate(
+        [
+            0.5 * grad_norm_attn, 0.5 * grad_norm_mlp, grad_gain_q, grad_gain_k,
+            jnp.full((128,), sq_local), jnp.zeros((640,), F32),
+        ]
+    ).reshape(24, 128)
+    down, gate, up, out, qkv, small = end(s_down, s_gate, s_up, p_out, p_qkv, small)
+
+    def columns(both, size):
+        both = both.reshape(2, both.shape[1], 4, -1)
+        return both.transpose(1, 2, 0, 3).reshape(both.shape[1], -1).astype(F32)
+
+    def mine(values):
+        size = values.shape[0] // 4
+        return lax.dynamic_slice_in_dim(values, f * size, size, 0)
+
+    qkv = qkv.reshape(2, -1, heads, HEAD_COLUMNS)
+    q_end = GROUP * HEAD_SIZE
+    output = lax.dynamic_slice_in_dim(fin.astype(BF16), k * rows, rows, 0)
+    return (
+        output[None],
+        small[18, 0] / count_total,
+        grad_input[None],
+        mine(small[0:8].reshape(-1)),
+        columns(qkv[..., :q_end], 0),
+        columns(qkv[..., q_end : q_end + HEAD_SIZE], 0),
+        columns(qkv[..., q_end + HEAD_SIZE :], 0),
+        mine(small[16]),
+        mine(small[17]),
+        out.reshape(-1, width).astype(F32),
+        mine(small[8:16].reshape(-1)),
+        columns(gate, 0),
+        columns(up, 0),
+        down.reshape(-1, width).astype(F32),
+    )
+
+
 def solution(mesh):
+    chips = mesh.shape["fsdp"] == 4 and mesh.shape["ctx"] == KEY_VALUE_HEADS
     return jax.shard_map(
-        per_device,
+        chip_step if chips else per_device,
         mesh=mesh,
         in_specs=(
             P("fsdp", "ctx", None),

time: 2020 us -> 751 us (0.37)
  waiting for transfers between devices: 1330 us -> 0 us
  Pallas kernels: 0 us -> 553 us
  matrix products: 258 us -> 50.4 us
  blocking collectives: 165 us -> 0 us
  local copies, waits for them, and re-layouts: 148 us -> 93.9 us
  other arithmetic: 77.9 us -> 38.6 us
    reduce_scatter x7 -> x0, waiting for transfers between devices: 906 us -> none  [the longest x1 160 us: per_device(): lax.psum_scatter(grads[9], ('fsdp', 'ctx'), scatter_dimension=0, tiled=True)]
    pallas_call x0 -> x12, Pallas kernels: none -> 553 us  [the longest x10 510 us: transfer(): pl.pallas_call(kernel, out_shape=outs, in_specs=in_specs, out_specs=out_s...]
    all_gather x14 -> x0, waiting for transfers between devices: 421 us -> none  [the longest x1 151 us: per_device(): lax.all_gather(query_pair, 'ctx', axis=0, tiled=True)]
    dot_general x35 -> x5, matrix products: 201 us -> 17 us  [the longest x1 4.6 us: chip_step(): projected = jnp.dot(hidden_one, w_qkv, preferred_element_type=F32)]
    psum x2 -> x0, blocking collectives: 79.1 us -> none  [per_device(): sq_total, count_total = lax.psum((sq_local, count_local), ('fsdp', 'ctx'))]
    all_gather x5 -> x0, blocking collectives: 61.8 us -> none  [the longest x1 15.3 us: per_device(): lax.all_gather(shares[2].astype(jnp.bfloat16), 'ctx', axis=0, tiled=True)]
    convert_element_type x0 -> x14, local copies, waits for them, and re-layouts: none -> 55.8 us  [the longest x12 49.3 us: columns(): return both.transpose(1, 2, 0, 3).reshape(both.shape[1], -1).astype(F32)]
    dynamic_slice x20 -> x6, local copies, waits for them, and re-layouts: 51.4 us -> 2.58 us  [the longest x4 2.43 us: mine(): return lax.dynamic_slice_in_dim(values, f * size, size, 0)]
  transfers between devices with their start and end apart: 21 -> 0, of which waited for: 14 -> 0; matrix products, arithmetic and copies ran while one was open for 17% -> 0% of each run, Pallas kernels for 0% -> 0%
where the time goes in v1:
time: 751 us; the launch traced here: 742 us
  Pallas kernels  553 us (74%)
  local copies, waits for them, and re-layouts  93.9 us (13%)
  matrix products  50.4 us (7%)
  other arithmetic  38.6 us (5%)
    pallas_call x10, Pallas kernels, transfer(): pl.pallas_call(kernel, out_shape=outs, in_specs=in_specs, out_specs=out_s...  510 us
    convert_element_type x12, local copies, waits for them, and re-layouts, columns(): return both.transpose(1, 2, 0, 3).reshape(both.shape[1], -1).astype(F32)  49.3 us
    pallas_call x1, Pallas kernels, attend_back(): pl.pallas_call(attend_back_kernel, out_shape=shape(qkv.shape, BF16), in_s...  24.1 us
    dot_general x5, matrix products, contract_rows(): lax.dot_general(left_arr, right_arr, (((0,), (0,)), ((), ())), preferred_...  19.5 us
    pallas_call x1, Pallas kernels, attend(): pl.pallas_call(attend_kernel, out_shape=[shape((tokens, GROUP * HEAD_SIZE...  18.5 us
    unnamed x80, local copies, waits for them, and re-layouts  15.3 us

profile of v1, /device:TPU:0, one launch (start us, length us, event | category | flops | bytes accessed | tf_op | source)
XLA Modules:
  0.0 741.9 jit_solution(14964416042331836597)
XLA Ops:
  0.7 2.8 concatenate.26
  4.1 1.4 add_convert_fusion.3.misc
  8.0 76.4 %begin.1 = (bf16[4,256,2048]{2,1,0:T(8,128)(2,1)}, bf16[2,256,1024]{2,1,0:T(8,128)(2,1)}, bf16[2,256,1024]{2,1,0:T(8,128)(2,1)}, f32[2,8,128]{2,1,0:T(8,128)}, f32[4,8,128]{2,1,0:T(8,128)}, /*index=5*/f32[8,128]{1,0:T(8,128)}) custom-call(bf16[256,2048]{1,0:T(8,128)(2,1)} %wq.1, bf16[256,1024]{1,0:T(8,128)(2,1)} %wk.1, bf16[256,1024]{1,0:T(8,128)(2,1)} %wv.1, ...), custom_call_target="tpu_custom_call" | custom-call | tf_op jit(solution)/shard_map/begin/pallas_call | solution.py:768
  84.4 1.5 multiply_reduce_fusion.8
  86.7 1.5 multiply_convert_fusion.3
  88.3 6.8 copy.29
  95.1 4.6 fusion.24
  99.7 2.0 copy-done
  103.2 2.2 multiply_multiply_fusion.1
  109.1 2.4 copy.39
  111.4 118.1 %to_heads.1 = (bf16[4,512,512]{2,1,0:T(8,128)(2,1)}, bf16[4,256,1536]{2,1,0:T(8,128)(2,1)}, bf16[4,256,1536]{2,1,0:T(8,128)(2,1)}) custom-call(bf16[4,512,512]{2,1,0:T(8,128)(2,1)} %bitcast.121, bf16[256,3072]{1,0:T(8,128)(2,1)} %wg.1, bf16[256,3072]{1,0:T(8,128)(2,1)} %wu.1), custom_call_target="tpu_custom_call" | custom-call | tf_op jit(solution)/shard_map/to_heads/pallas_call | solution.py:768
  229.6 18.5 %attend.1 = (bf16[2048,256]{1,0:T(8,128)(2,1)}, f32[2,8,2048]{2,1,0:T(8,128)}) custom-call(bf16[2048,512]{1,0:T(8,128)(2,1)} %bitcast.119), custom_call_target="tpu_custom_call" | custom-call | tf_op jit(solution)/shard_map/attend/pallas_call | solution.py:1190
  248.1 86.7 %to_tokens.1 = (bf16[512,1024]{1,0:T(8,128)(2,1)}, bf16[4,384,1024]{2,1,0:T(8,128)(2,1)}, bf16[4,256,1024]{2,1,0:T(8,128)(2,1)}) custom-call(bf16[2048,256]{1,0:T(8,128)(2,1)} %get-tuple-element.44.att, bf16[768,1024]{1,0:T(8,128)(2,1)} %wd.1, bf16[512,1024]{1,0:T(8,128)(2,1)} %wo.1), custom_call_target="tpu_custom_call" | custom-call | tf_op jit(solution)/shard_map/to_tokens/pallas_call | solution.py:768
  334.7 4.1 convolution_convert_fusion.7.src
  338.9 3.0 swap7.1
  341.9 1.8 multiply_reduce_fusion.7
  344.0 2.0 copy-done.27
  346.0 1.8 fusion.25
  347.9 3.6 multiply_convert_fusion.1
  352.6 2.8 convolution_convert_fusion.6.src
  355.5 3.0 swap8.1
  358.5 3.1 fusion.3
  363.9 1.6 copy-done.30
  365.4 3.7 multiply_convert_fusion
  369.2 3.5 convolution_convert_fusion.1
  372.7 3.5 convolution_convert_fusion.2
  376.2 3.5 convolution_convert_fusion.3
  379.7 1.8 fusion.26
  381.6 2.8 add_convert_fusion.2.src
  384.4 3.0 swap9.1
  387.4 2.0 multiply_reduce_fusion.4
  390.4 1.3 copy-done.9
  391.7 2.3 convolution_convert_fusion.5.grads
  394.0 29.7 %grads_to_heads.1 = (bf16[4,512,256]{2,1,0:T(8,128)(2,1)}, bf16[384,1024]{1,0:T(8,128)(2,1)}) custom-call(bf16[512,1024]{1,0:T(8,128)(2,1)} %convolution_convert_fusion.5.grads, bf16[4,384,1024]{2,1,0:T(8,128)(2,1)} %bitcast.127), custom_call_target="tpu_custom_call" | custom-call | tf_op jit(solution)/shard_map/grads_to_heads/pallas_call | solution.py:768
  423.7 24.1 %attend_back.1.grads = bf16[2048,512]{1,0:T(8,128)(2,1)} custom-call(bf16[2048,512]{1,0:T(8,128)(2,1)} %bitcast.120, bf16[2048,256]{1,0:T(8,128)(2,1)} %get-tuple-element.44.att, bf16[2048,256]{1,0:T(8,128)(2,1)} %bitcast.133, f32[2,8,2048]{2,1,0:T(8,128)} %get-tuple-element.54.lse), custom_call_target="tpu_custom_call" | custom-call | tf_op jit(solution)/shard_map/attend_back/pallas_call | solution.py:1244
  447.7 56.0 %grads_to_tokens.1 = (bf16[512,2048]{1,0:T(8,128)(2,1)}, bf16[256,1536]{1,0:T(8,128)(2,1)}, bf16[256,1536]{1,0:T(8,128)(2,1)}) custom-call(bf16[2048,512]{1,0:T(8,128)(2,1)} %attend_back.1.grads, bf16[4,256,1536]{2,1,0:T(8,128)(2,1)} %bitcast.129, bf16[4,256,1536]{2,1,0:T(8,128)(2,1)} %bitcast.128), custom_call_target="tpu_custom_call" | custom-call | tf_op jit(solution)/shard_map/grads_to_tokens/pallas_call | solution.py:768
  503.8 4.2 copy.40
  507.9 2.5 slice_multiply_fusion
  511.1 1.6 copy-done.2
  512.8 1.7 multiply_reduce_fusion
  518.4 3.3 convolution_convert_fusion.8.src
  521.8 3.0 swap10.1
  524.8 3.4 multiply_reduce_fusion.3
  529.0 6.4 convolution_convert_fusion
  535.4 2.6 convolution_convert_fusion.4
  538.0 131.3 %end.1 = (bf16[2,384,1024]{2,1,0:T(8,128)(2,1)}, bf16[2,256,1536]{2,1,0:T(8,128)(2,1)}, bf16[2,256,1536]{2,1,0:T(8,128)(2,1)}, bf16[2,256,1024]{2,1,0:T(8,128)(2...) custom-call(bf16[384,1024]{1,0:T(8,128)(2,1)} %get-tuple-element.52.down, ...), custom_call_target="tpu_custom_call" | custom-call | tf_op jit(solution)/shard_map/end/pallas_call | solution.py:768
  669.4 4.5 reshape.277
  673.9 6.0 copy.36
  679.8 5.5 reshape.274
  685.3 4.3 reshape.278
  689.6 6.0 copy.37
  695.5 5.5 reshape.275
  701.0 4.7 reshape.264
  705.7 1.5 convert_bitcast_fusion
  707.2 2.9 copy.33
  710.1 3.9 reshape.270
  714.0 2.3 convert_bitcast_fusion.1
  716.3 1.8 copy.34
  718.1 3.0 reshape.271
  721.1 3.0 copy.35
  724.1 3.0 reshape.272
  728.8 2.6 fusion.7
  731.4 2.2 bitcast_convert_fusion
  733.5 1.6 bitcast_convert_fusion.1
  (127 shorter events, 22.6 us)
Async XLA Ops:
  88.2 6.9 copy-start.19
  99.7 2.0 copy-start
  105.5 0.7 copy-start.24
  105.5 2.2 copy-start.1
  106.8 2.0 copy-start.15
  338.9 3.0 copy-start.4
  338.9 3.0 copy-start.11
  343.7 2.3 copy-start.27
  344.0 3.8 copy-start.20
  346.0 1.9 copy-start.25
  347.8 3.7 copy-start.33
  347.9 4.8 copy-start.29
  351.5 1.1 copy-start.35
  355.5 3.0 copy-start.7
  355.5 3.0 copy-start.14
  358.5 5.3 copy-start.34
  358.5 5.3 copy-start.37
  363.5 1.9 copy-start.30
  365.4 3.7 copy-start.21
  372.7 3.5 copy-start.36
  376.2 3.5 copy-start.28
  379.7 1.9 copy-start.26
  384.4 3.0 copy-start.5
  387.4 2.1 copy-start.6
  389.5 2.2 copy-start.31
  390.3 1.3 copy-start.9
  507.9 3.2 copy-start.3
  510.4 2.4 copy-start.2
  515.5 2.9 copy-start.12
  515.8 1.3 copy-start.16
  521.8 3.1 copy-start.13
  529.0 6.4 copy-start.22
  529.0 6.4 copy-start.10
  529.0 6.4 copy-start.32
  727.2 1.6 copy-start.8
  728.8 2.6 copy-start.17
  731.4 2.2 copy-start.18
  733.5 1.6 copy-start.23

commit v2 on v1

--- a/solution.py
+++ b/solution.py
@@ -529,6 +529,11 @@
             copy.wait()
         self.open = []
 
+    def alone(self, src, dst):
+        copy = self(src, dst)
+        self.open.pop()
+        return copy
+
 
 def add_rows(dst, sources):
     rows = dst.shape[0]
@@ -544,14 +549,15 @@
 
 
 class Gather:
-    def __init__(self, me, copies, buf):
+    def __init__(self, me, copies, local, own, buf):
         half = buf.shape[1] // 2
         a, b = pl.ds(0, half), pl.ds(half, half)
         own_a, own_b = buf.at[me.f, a], buf.at[me.f, b]
-        self.a_x = copies(own_a, own_a, me.xp)
-        self.b_y = copies(own_b, own_b, me.yp)
-        self.b_x = copies(own_b, own_b, me.xp)
-        self.a_y = copies(own_a, own_a, me.yp)
+        self.local, self.own, self.slot = local, own, buf.at[me.f]
+        self.a_x = copies(own.at[a], own_a, me.xp)
+        self.b_y = copies(own.at[b], own_b, me.yp)
+        self.b_x = copies(own.at[b], own_b, me.xp)
+        self.a_y = copies(own.at[a], own_a, me.yp)
         self.on_y = copies(buf.at[me.fx, a], buf.at[me.fx, a], me.yp)
         self.on_x = copies(buf.at[me.fy, b], buf.at[me.fy, b], me.xp)
 
@@ -562,6 +568,7 @@
     def second(self):
         self.b_x.start()
         self.a_y.start()
+        self.kept = self.local.alone(self.own, self.slot)
 
     def relay(self):
         self.a_x.wait_recv()
@@ -574,6 +581,7 @@
             copy.wait_recv()
         for copy in (self.a_x, self.b_y, self.b_x, self.a_y, self.on_y, self.on_x):
             copy.wait_send()
+        self.kept.wait()
 
 
 def scatter_buffers(rows, columns):
@@ -790,7 +798,7 @@
 def kernel_begin(
     wq, wk, wv, x, t, misc, gains, count,
     w_all, x_pair, t_pair, misc_pair, gains_all, count_out,
-    plane, line, send, recv, lsem,
+    own, plane, line, send, recv, lsem,
 ):
     me = Place()
     ctx = [me.along_ctx(step)[1] for step in range(1, 8)]
@@ -802,9 +810,9 @@
         at = HEAD_COLUMNS * i
         q_at = pl.ds(pl.multiple_of(head * q, HEAD_SIZE), q)
         k_at = pl.ds(pl.multiple_of(head * HEAD_SIZE, HEAD_SIZE), HEAD_SIZE)
-        local(wq.at[:, q_at], w_all.at[me.f, :, pl.ds(at, q)])
-        local(wk.at[:, k_at], w_all.at[me.f, :, pl.ds(at + q, HEAD_SIZE)])
-        local(wv.at[:, k_at], w_all.at[me.f, :, pl.ds(at + q + HEAD_SIZE, HEAD_SIZE)])
+        local(wq.at[:, q_at], own.at[:, pl.ds(at, q)])
+        local(wk.at[:, k_at], own.at[:, pl.ds(at + q, HEAD_SIZE)])
+        local(wv.at[:, k_at], own.at[:, pl.ds(at + q + HEAD_SIZE, HEAD_SIZE)])
     small = SmallSum(me, copies, count, plane, line)
     small.first()
     others = [copies(gains, gains_all.at[me.f], partner) for partner in (me.xp, me.yp, me.dp)]
@@ -813,7 +821,7 @@
     for copy in others:
         copy.start()
     local.wait()
-    weights = Gather(me, copies, w_all)
+    weights = Gather(me, copies, local, own, w_all)
     weights.first()
     weights.second()
     for src, dst in ((x, x_pair), (t, t_pair), (misc, misc_pair)):
@@ -837,7 +845,7 @@
     return transfer(
         kernel_begin, "begin", 1,
         (wq, wk, wv, x, t, misc, gains, count),
-        [HBM] * 7 + [VM],
+        [HBM] * 3 + [VM] * 5,
         [
             shape((4, rows, columns), BF16),
             shape((2,) + x.shape, BF16),
@@ -847,14 +855,14 @@
             shape((8, 128), F32),
         ],
         [HBM] * 5 + [VM],
-        [pltpu.VMEM((4, 8, 128), F32), pltpu.VMEM((8, 8, 128), F32)],
+        [pltpu.VMEM((rows, columns), BF16), pltpu.VMEM((4, 8, 128), F32), pltpu.VMEM((8, 8, 128), F32)],
         24, 20,
     )
 
 
 class Exchange:
-    def __init__(self, me, copies, local, piece, place):
-        self.me, self.local, self.piece, self.place = me, local, piece, place
+    def __init__(self, me, copies, local, stage, piece, place):
+        self.me, self.local, self.piece, self.place, self.stage = me, local, piece, place, stage
         self.sends = []
         for step in (2, 1, 3):
             other, partner = me.along_z(step)
@@ -863,7 +871,11 @@
     def start(self):
         for copy in self.sends:
             copy.start()
-        self.own = self.local(self.piece(self.me.z), self.place(self.me.z))
+        self.own = self.local.alone(self.piece(self.me.z), self.stage)
+
+    def pass_own(self):
+        self.own.wait()
+        self.own = self.local.alone(self.stage, self.place(self.me.z))
 
     def finish(self):
         self.own.wait()
@@ -871,28 +883,30 @@
             copy.wait()
 
 
-def kernel_to_heads(qkv, wg, wu, qkv_all, wg_all, wu_all, send, recv, lsem):
+def kernel_to_heads(qkv, wg, wu, qkv_all, wg_all, wu_all, stage, own_g, own_u, send, recv, lsem):
     me = Place()
     greet([me.xp, me.yp] + [me.along_z(step)[1] for step in (1, 2, 3)])
-    copies, local, second = Copies(send, recv), Locals(lsem), Locals(lsem)
+    copies, local = Copies(send, recv), Locals(lsem)
     move = Exchange(
-        me, copies, local, lambda z: qkv.at[z], lambda z: qkv_all.at[z]
+        me, copies, local, stage, lambda z: qkv.at[z], lambda z: qkv_all.at[z]
     )
     move.start()
-    second.used = 1
     width = wg.shape[1] // 8
-    for src, dst in ((wg, wg_all), (wu, wu_all)):
+    for src, own in ((wg, own_g), (wu, own_u)):
         for i in range(4):
             at = pl.ds(pl.multiple_of((2 * i + me.k) * width, 128), width)
-            second(src.at[:, at], dst.at[me.f, :, pl.ds(i * width, width)])
-    second.wait()
-    gathers = [Gather(me, copies, wg_all), Gather(me, copies, wu_all)]
+            local(src.at[:, at], own.at[:, pl.ds(i * width, width)])
+    local.wait()
+    gathers = [
+        Gather(me, copies, local, own_g, wg_all), Gather(me, copies, local, own_u, wu_all)
+    ]
     for gather in gathers:
         gather.first()
     for gather in gathers:
         gather.second()
     for gather in gathers:
         gather.relay()
+    move.pass_own()
     move.finish()
     for gather in gathers:
         gather.finish()
@@ -908,33 +922,37 @@
             shape((4, rows, columns // 2), BF16),
             shape((4, rows, columns // 2), BF16),
         ],
-        [HBM] * 3, [], 15, 9,
-    )
-
-
-def kernel_to_tokens(att, wd, wo, att_all, wd_all, wo_all, send, recv, lsem):
+        [HBM] * 3,
+        [pltpu.VMEM(qkv.shape[1:], BF16)] + [pltpu.VMEM((rows, columns // 2), BF16)] * 2,
+        15, 12,
+    )
+
+
+def kernel_to_tokens(att, wd, wo, att_all, wd_all, wo_all, stage, own_d, own_o, send, recv, lsem):
     me = Place()
     greet([me.xp, me.yp] + [me.along_z(step)[1] for step in (1, 2, 3)])
-    copies, local, second = Copies(send, recv), Locals(lsem), Locals(lsem)
+    copies, local = Copies(send, recv), Locals(lsem)
     tokens, width = att_all.shape[0], att.shape[1]
-    second.used = 1
-    for src, dst in ((wd, wd_all), (wo, wo_all)):
-        rows = dst.shape[1]
-        second(src.at[pl.ds(pl.multiple_of(me.k * rows, 16), rows)], dst.at[me.f])
+    for src, own in ((wd, own_d), (wo, own_o)):
+        rows = own.shape[0]
+        local(src.at[pl.ds(pl.multiple_of(me.k * rows, 16), rows)], own)
     move = Exchange(
-        me, copies, local,
+        me, copies, local, stage,
         lambda z: att.at[pl.ds(pl.multiple_of(z * tokens, 16), tokens)],
         lambda z: att_all.at[:, pl.ds(pl.multiple_of(z * width, 128), width)],
     )
     move.start()
-    second.wait()
-    gathers = [Gather(me, copies, wo_all), Gather(me, copies, wd_all)]
+    local.wait()
+    gathers = [
+        Gather(me, copies, local, own_o, wo_all), Gather(me, copies, local, own_d, wd_all)
+    ]
     for gather in gathers:
         gather.first()
     for gather in gathers:
         gather.second()
     for gather in gathers:
         gather.relay()
+    move.pass_own()
     move.finish()
     for gather in gathers:
         gather.finish()
@@ -949,7 +967,13 @@
             shape((4, wd.shape[0] // 2, wd.shape[1]), BF16),
             shape((4, wo.shape[0] // 2, wo.shape[1]), BF16),
         ],
-        [HBM] * 3, [], 15, 3,
+        [HBM] * 3,
+        [
+            pltpu.VMEM((att.shape[0] // 4, att.shape[1]), BF16),
+            pltpu.VMEM((wd.shape[0] // 2, wd.shape[1]), BF16),
+            pltpu.VMEM((wo.shape[0] // 2, wo.shape[1]), BF16),
+        ],
+        15, 6,
     )
 
 
@@ -975,6 +999,7 @@
         scatter.second()
     for scatter in scatters:
         scatter.relay()
+    move.pass_own()
     writes = []
     for scatter, out in zip(scatters, outs):
         scatter.finish(scatter.sum_a, scatter.sum_b)
@@ -988,13 +1013,13 @@
         write.wait()
 
 
-def kernel_grads_to_heads(grads, down, grads_all, down_sum, bufs, send, recv, lsem):
+def kernel_grads_to_heads(grads, down, grads_all, down_sum, stage, bufs, send, recv, lsem):
     me = Place()
     greet([me.xp, me.yp] + [me.along_z(step)[1] for step in (1, 2, 3)])
     copies, local = Copies(send, recv), Locals(lsem)
     width = grads_all.shape[2]
     move = Exchange(
-        me, copies, local,
+        me, copies, local, stage,
         lambda z: grads.at[:, pl.ds(pl.multiple_of(z * width, 128), width)],
         lambda z: grads_all.at[z],
     )
@@ -1007,17 +1032,18 @@
         kernel_grads_to_heads, "grads_to_heads", 4,
         (grads, down), [HBM] * 2,
         [shape((4, tokens, columns // 4), BF16), shape(down.shape[1:], BF16)],
-        [HBM] * 2, scatter_buffers(*down.shape[1:]), 9, 7,
-    )
-
-
-def kernel_grads_to_tokens(grads, gate, up, grads_all, gate_sum, up_sum, bufs_g, bufs_u, send, recv, lsem):
+        [HBM] * 2,
+        [pltpu.VMEM((tokens, columns // 4), BF16)] + scatter_buffers(*down.shape[1:]), 9, 8,
+    )
+
+
+def kernel_grads_to_tokens(grads, gate, up, grads_all, gate_sum, up_sum, stage, bufs_g, bufs_u, send, recv, lsem):
     me = Place()
     greet([me.xp, me.yp] + [me.along_z(step)[1] for step in (1, 2, 3)])
     copies, local = Copies(send, recv), Locals(lsem)
     tokens, width = grads_all.shape[0], grads.shape[1]
     move = Exchange(
-        me, copies, local,
+        me, copies, local, stage,
         lambda z: grads.at[pl.ds(pl.multiple_of(z * tokens, 16), tokens)],
         lambda z: grads_all.at[:, pl.ds(pl.multiple_of(z * width, 128), width)],
     )
@@ -1038,7 +1064,10 @@
             shape(up.shape[1:], BF16),
         ],
         [HBM] * 3,
-        scatter_buffers(*gate.shape[1:]) + scatter_buffers(*up.shape[1:]), 15, 13,
+        [pltpu.VMEM((grads.shape[0] // 4, grads.shape[1]), BF16)]
+        + scatter_buffers(*gate.shape[1:])
+        + scatter_buffers(*up.shape[1:]),
+        15, 14,
     )
 
 
@@ -1140,6 +1169,49 @@
     )
 
 
+def assemble_kernel(gate, up, qkv, down, out, g_gate, g_up, g_q, g_k, g_v, g_down, g_out):
+    for src, dst in ((gate, g_gate), (up, g_up)):
+        width = src.shape[2] // 4
+        for i in range(4):
+            for j in range(2):
+                dst[:, pl.ds((2 * i + j) * width, width)] = src[j, :, pl.ds(i * width, width)].astype(F32)
+    q_size, size = GROUP * HEAD_SIZE, HEAD_SIZE
+    for i in range(4):
+        for j in range(2):
+            head, at = 2 * i + j, HEAD_COLUMNS * i
+            g_q[:, pl.ds(head * q_size, q_size)] = qkv[j, :, pl.ds(at, q_size)].astype(F32)
+            g_k[:, pl.ds(head * size, size)] = qkv[j, :, pl.ds(at + q_size, size)].astype(F32)
+            g_v[:, pl.ds(head * size, size)] = qkv[j, :, pl.ds(at + q_size + size, size)].astype(F32)
+    g_down[...] = down[...].astype(F32)
+    g_out[...] = out[...].astype(F32)
+
+
+def assemble(gate, up, qkv, down, out):
+    steps = 8
+
+    def cut(dims):
+        return pl.BlockSpec((2, dims[1] // steps, dims[2]), lambda i: (0, i, 0))
+
+    def flat(rows, columns):
+        return pl.BlockSpec((rows // steps, columns), lambda i: (i, 0)), shape((rows, columns), F32)
+
+    rows, width = gate.shape[1], 2 * gate.shape[2]
+    heads = KEY_VALUE_HEADS * HEAD_SIZE
+    outs = [
+        flat(rows, width), flat(rows, width), flat(rows, GROUP * heads), flat(rows, heads), flat(rows, heads),
+        (cut(down.shape), shape(down.shape, F32)), (cut(out.shape), shape(out.shape, F32)),
+    ]
+    return pl.pallas_call(
+        assemble_kernel,
+        grid=(steps,),
+        out_shape=[s for _, s in outs],
+        in_specs=[cut(a.shape) for a in (gate, up, qkv, down, out)],
+        out_specs=[b for b, _ in outs],
+        compiler_params=pltpu.CompilerParams(vmem_limit_bytes=VMEM_LIMIT),
+        name="assemble",
+    )(gate, up, qkv, down, out)
+
+
 def dot_nt(a, b, **kw):
     return lax.dot_general(a, b, (((1,), (1,)), ((), ())), preferred_element_type=F32, **kw)
 
@@ -1359,32 +1431,27 @@
     ).reshape(24, 128)
     down, gate, up, out, qkv, small = end(s_down, s_gate, s_up, p_out, p_qkv, small)
 
-    def columns(both, size):
-        both = both.reshape(2, both.shape[1], 4, -1)
-        return both.transpose(1, 2, 0, 3).reshape(both.shape[1], -1).astype(F32)
-
     def mine(values):
         size = values.shape[0] // 4
         return lax.dynamic_slice_in_dim(values, f * size, size, 0)
 
-    qkv = qkv.reshape(2, -1, heads, HEAD_COLUMNS)
-    q_end = GROUP * HEAD_SIZE
+    g_gate, g_up, g_q, g_k, g_v, g_down, g_out = assemble(gate, up, qkv, down, out)
     output = lax.dynamic_slice_in_dim(fin.astype(BF16), k * rows, rows, 0)
     return (
         output[None],
         small[18, 0] / count_total,
         grad_input[None],
         mine(small[0:8].reshape(-1)),
-        columns(qkv[..., :q_end], 0),
-        columns(qkv[..., q_end : q_end + HEAD_SIZE], 0),
-        columns(qkv[..., q_end + HEAD_SIZE :], 0),
+        g_q,
+        g_k,
+        g_v,
         mine(small[16]),
         mine(small[17]),
-        out.reshape(-1, width).astype(F32),
+        g_out.reshape(-1, width),
         mine(small[8:16].reshape(-1)),
-        columns(gate, 0),
-        columns(up, 0),
-        down.reshape(-1, width).astype(F32),
+        g_gate,
+        g_up,
+        g_down.reshape(-1, width),
     )
 
 

time: 751 us -> 564 us (0.75)
  Pallas kernels: 553 us -> 429 us
  local copies, waits for them, and re-layouts: 93.9 us -> 38.7 us
  other arithmetic: 38.6 us -> 30.9 us
    pallas_call x10, Pallas kernels: 510 us -> 377 us  [transfer(): pl.pallas_call(kernel, out_shape=outs, in_specs=in_specs, out_specs=out_s...]
    convert_element_type x12 -> x0, local copies, waits for them, and re-layouts: 49.3 us -> none  [columns(): return both.transpose(1, 2, 0, 3).reshape(both.shape[1], -1).astype(F32)]
    pallas_call x0 -> x1, Pallas kernels: none -> 9.85 us  [assemble(): pl.pallas_call(assemble_kernel, grid=(steps,), out_shape=[s for _, s in o...]
    convert_element_type x4 -> x0, other arithmetic: 7.59 us -> none  [the longest x2 3.8 us: columns(): return both.transpose(1, 2, 0, 3).reshape(both.shape[1], -1).astype(F32)]
    unnamed x80 -> x78, local copies, waits for them, and re-layouts: 15.3 us -> 14.2 us
where the time goes in v2:
time: 564 us; the launch traced here: 555 us
  Pallas kernels  429 us (76%)
  matrix products  50.4 us (9%)
  local copies, waits for them, and re-layouts  38.7 us (7%)
  other arithmetic  30.9 us (5%)
  between operations  5.92 us (1%)
    pallas_call x10, Pallas kernels, transfer(): pl.pallas_call(kernel, out_shape=outs, in_specs=in_specs, out_specs=out_s...  377 us
    pallas_call x1, Pallas kernels, attend_back(): pl.pallas_call(attend_back_kernel, out_shape=shape(qkv.shape, BF16), in_s...  24.1 us
    dot_general x5, matrix products, contract_rows(): lax.dot_general(left_arr, right_arr, (((0,), (0,)), ((), ())), preferred_...  19.5 us
    pallas_call x1, Pallas kernels, attend(): pl.pallas_call(attend_kernel, out_shape=[shape((tokens, GROUP * HEAD_SIZE...  18.5 us
    unnamed x78, local copies, waits for them, and re-layouts  14.2 us
    dot_general x5, matrix products, against(): lax.dot_general(left_arr, right_arr, (((1,), (1,)), ((), ())), preferred_...  13.9 us

profile of v2, /device:TPU:0, one launch (start us, length us, event | category | flops | bytes accessed | tf_op | source)
XLA Modules:
  0.0 555.0 jit_solution(16925087125738504578)
XLA Ops:
  0.7 2.8 concatenate.26
  3.4 0.6 bitcast_convert_fusion.gains
  4.1 1.4 add_convert_fusion.3.misc
  5.4 1.3 reduce_sum.107
  7.4 0.6 broadcast_in_dim.42.count
  8.0 45.2 %begin.1 = (bf16[4,256,2048]{2,1,0:T(8,128)(2,1)}, bf16[2,256,1024]{2,1,0:T(8,128)(2,1)}, bf16[2,256,1024]{2,1,0:T(8,128)(2,1)}, f32[2,8,128]{2,1,0:T(8,128)}, f32[4,8,128]{2,1,0:T(8,128)}, /*index=5*/f32[8,128]{1,0:T(8,128)}) custom-call(bf16[256,2048]{1,0:T(8,128)(2,1)} %wq.1, bf16[256,1024]{1,0:T(8,128)(2,1)} %wk.1, bf16[256,1024]{1,0:T(8,128)(2,1)} %wv.1, ...), custom_call_target="tpu_custom_call" | custom-call | tf_op jit(solution)/shard_map/begin/pallas_call | solution.py:776
  53.2 1.5 multiply_reduce_fusion.8
  54.7 0.8 fusion.21
  55.5 1.5 multiply_convert_fusion.3
  57.1 6.8 %copy.29 = bf16[2048,1024]{1,0:T(8,128)(2,1)} copy(bf16[2048,1024]{0,1:T(8,128)(2,1)} %bitcast.109) | data formatting | bytes 8388608 | tf_op jit(solution)/shard_map/dot_general | solution.py:1373
  63.9 4.6 fusion.24
  68.5 2.0 copy-done
  70.9 0.9 slice_reduce_fusion.1
  72.0 2.2 multiply_multiply_fusion.1
  75.6 0.9 copy-done.1
  76.5 1.1 fusion.1
  77.9 2.4 copy.34
  80.2 54.9 %to_heads.1 = (bf16[4,512,512]{2,1,0:T(8,128)(2,1)}, bf16[4,256,1536]{2,1,0:T(8,128)(2,1)}, bf16[4,256,1536]{2,1,0:T(8,128)(2,1)}) custom-call(bf16[4,512,512]{2,1,0:T(8,128)(2,1)} %bitcast.107, bf16[256,3072]{1,0:T(8,128)(2,1)} %wg.1, bf16[256,3072]{1,0:T(8,128)(2,1)} %wu.1), custom_call_target="tpu_custom_call" | custom-call | tf_op jit(solution)/shard_map/to_heads/pallas_call | solution.py:776
  135.1 18.5 %attend.1 = (bf16[2048,256]{1,0:T(8,128)(2,1)}, f32[2,8,2048]{2,1,0:T(8,128)}) custom-call(bf16[2048,512]{1,0:T(8,128)(2,1)} %bitcast.105), custom_call_target="tpu_custom_call" | custom-call | tf_op jit(solution)/shard_map/attend/pallas_call | solution.py:1262
  153.6 47.1 %to_tokens.1 = (bf16[512,1024]{1,0:T(8,128)(2,1)}, bf16[4,384,1024]{2,1,0:T(8,128)(2,1)}, bf16[4,256,1024]{2,1,0:T(8,128)(2,1)}) custom-call(bf16[2048,256]{1,0:T(8,128)(2,1)} %get-tuple-element.51.att, bf16[768,1024]{1,0:T(8,128)(2,1)} %wd.1, bf16[512,1024]{1,0:T(8,128)(2,1)} %wo.1), custom_call_target="tpu_custom_call" | custom-call | tf_op jit(solution)/shard_map/to_tokens/pallas_call | solution.py:776
  200.7 4.1 convolution_convert_fusion.7.src
  204.8 3.0 swap7.1
  207.9 1.8 multiply_reduce_fusion.7
  209.9 2.0 copy-done.26
  211.9 1.8 fusion.25
  213.8 3.6 multiply_convert_fusion.1
  217.4 2.8 convolution_convert_fusion.6.src
  220.2 3.0 swap8.1
  223.3 3.1 fusion.3
  226.4 1.2 slice.60
  228.6 1.6 copy-done.29
  230.2 3.7 multiply_convert_fusion
  233.9 3.5 convolution_convert_fusion.1
  237.4 3.5 convolution_convert_fusion.2
  240.9 3.5 convolution_convert_fusion.3
  244.4 1.8 fusion.26
  246.3 2.8 add_convert_fusion.2.src
  249.1 3.0 swap9.1
  252.2 2.1 multiply_reduce_fusion.4
  254.3 0.9 fusion.2
  255.2 1.3 copy-done.10
  256.5 2.3 convolution_convert_fusion.5.grads
  258.8 29.7 %grads_to_heads.1 = (bf16[4,512,256]{2,1,0:T(8,128)(2,1)}, bf16[384,1024]{1,0:T(8,128)(2,1)}) custom-call(bf16[512,1024]{1,0:T(8,128)(2,1)} %convolution_convert_fusion.5.grads, bf16[4,384,1024]{2,1,0:T(8,128)(2,1)} %bitcast.113), custom_call_target="tpu_custom_call" | custom-call | tf_op jit(solution)/shard_map/grads_to_heads/pallas_call | solution.py:776
  288.5 24.1 %attend_back.1.grads = bf16[2048,512]{1,0:T(8,128)(2,1)} custom-call(bf16[2048,512]{1,0:T(8,128)(2,1)} %bitcast.106, bf16[2048,256]{1,0:T(8,128)(2,1)} %get-tuple-element.51.att, bf16[2048,256]{1,0:T(8,128)(2,1)} %bitcast.119, f32[2,8,2048]{2,1,0:T(8,128)} %get-tuple-element.61.lse), custom_call_target="tpu_custom_call" | custom-call | tf_op jit(solution)/shard_map/attend_back/pallas_call | solution.py:1316
  312.6 56.1 %grads_to_tokens.1 = (bf16[512,2048]{1,0:T(8,128)(2,1)}, bf16[256,1536]{1,0:T(8,128)(2,1)}, bf16[256,1536]{1,0:T(8,128)(2,1)}) custom-call(bf16[2048,512]{1,0:T(8,128)(2,1)} %attend_back.1.grads, bf16[4,256,1536]{2,1,0:T(8,128)(2,1)} %bitcast.115, bf16[4,256,1536]{2,1,0:T(8,128)(2,1)} %bitcast.114), custom_call_target="tpu_custom_call" | custom-call | tf_op jit(solution)/shard_map/grads_to_tokens/pallas_call | solution.py:776
  368.6 4.2 copy.35
  372.8 2.5 slice_multiply_fusion
  376.0 1.6 copy-done.2
  377.6 1.7 multiply_reduce_fusion
  379.3 0.9 add_add_fusion
  380.7 1.3 copy-done.17
  382.0 1.3 copy-done.13
  383.3 3.4 convolution_convert_fusion.8.src
  386.6 3.0 swap10.1
  389.7 3.4 multiply_reduce_fusion.3
  393.9 6.4 %convolution_convert_fusion = bf16[1024,2048]{1,0:T(8,128)(2,1)} fusion(bf16[512,1024]{1,0:T(8,128)(2,1)} %bitcast.121, bf16[512,2048]{0,1:T(8,128)(2,1)} %bitcast.117), kind=kOutput, calls=%fused_computation.2 | convolution fusion | flops 2149580800 | bytes 7340032 | tf_op jit(solution)/shard_map/dot_general | solution.py:65
  400.3 2.6 convolution_convert_fusion.4
  402.9 131.6 %end.1 = (bf16[2,384,1024]{2,1,0:T(8,128)(2,1)}, bf16[2,256,1536]{2,1,0:T(8,128)(2,1)}, bf16[2,256,1536]{2,1,0:T(8,128)(2,1)}, bf16[2,256,1024]{2,1,0:T(8,128)(2...) custom-call(bf16[384,1024]{1,0:T(8,128)(2,1)} %get-tuple-element.59.down, ...), custom_call_target="tpu_custom_call" | custom-call | tf_op jit(solution)/shard_map/end/pallas_call | solution.py:776
  534.6 9.9 %assemble.1 = (f32[256,3072]{1,0:T(8,128)}, f32[256,3072]{1,0:T(8,128)}, f32[256,2048]{1,0:T(8,128)}, f32[256,1024]{1,0:T(8,128)}, f32[256,1024]{1,0:T(8,128)}, ...) custom-call(bf16[2,256,1536]{2,1,0:T(8,128)(2,1)} %get-tuple-element.66.gate, ...), custom_call_target="tpu_custom_call" | custom-call | tf_op jit(solution)/shard_map/assemble/pallas_call | solution.py:1204
  544.9 1.1 copy-done.9
  546.0 2.5 fusion.7
  548.5 0.6 dynamic_slice.24
  549.2 0.6 dynamic_slice.29
  552.8 0.9 fusion.8
  (109 shorter events, 6.4 us)
Async XLA Ops:
  57.0 6.8 %copy-start.18 = (bf16[2,256,1024]{2,1,0:T(8,128)(2,1)}, bf16[2,256,1024]{2,1,0:T(8,128)(2,1)S(1)}, u32[]{:S(2)}) copy-start(bf16[2,256,1024]{2,1,0:T(8,128)(2,1)S(1)} %multiply_convert_fusion.3) | copy-start | bytes 3145732
  68.5 2.0 copy-start
  74.2 0.7 copy-start.23
  74.3 2.2 copy-start.1
  75.6 2.0 copy-start.16
  204.8 3.0 copy-start.4
  204.8 3.0 copy-start.12
  209.7 2.3 copy-start.26
  209.9 3.8 copy-start.19
  211.9 1.9 copy-start.24
  213.7 3.7 copy-start.32
  213.8 3.6 copy-start.28
  217.4 2.8 copy-start.34
  220.2 3.0 copy-start.7
  220.2 3.0 copy-start.15
  223.3 5.3 copy-start.33
  223.3 5.3 copy-start.36
  228.3 1.9 copy-start.29
  230.2 3.7 copy-start.20
  237.4 3.5 copy-start.35
  240.9 3.5 copy-start.27
  244.4 1.9 copy-start.25
  249.1 3.0 copy-start.5
  252.1 2.1 copy-start.6
  252.2 2.1 copy-start.8
  254.3 2.2 copy-start.30
  255.2 1.3 copy-start.10
  372.8 3.2 copy-start.3
  375.3 2.4 copy-start.2
  380.3 2.9 copy-start.13
  380.7 1.3 copy-start.17
  386.6 3.1 copy-start.14
  393.9 6.4 %copy-start.21 = (f32[3072]{0:T(1024)}, f32[3072]{0:T(1024)S(1)}, u32[]{:S(2)}) copy-start(f32[3072]{0:T(1024)S(1)} %constant_dynamic-update-slice_fusion) | copy-start | bytes 36868
  393.9 6.4 %copy-start.11 = (f32[512,1024]{1,0:T(8,128)S(1)}, f32[512,1024]{1,0:T(8,128)}, u32[]{:S(2)}) copy-start(f32[512,1024]{1,0:T(8,128)} %copy-done.10) | copy-start | bytes 6291460
  393.9 6.4 %copy-start.31 = (bf16[512,1024]{1,0:T(8,128)(2,1)S(1)}, bf16[512,1024]{1,0:T(8,128)(2,1)}, u32[]{:S(2)}) copy-start(bf16[512,1024]{1,0:T(8,128)(2,1)} %get-tuple-element.52) | copy-start | bytes 3145732
  544.4 1.6 copy-start.9
  546.0 2.5 copy-start.22
